TPU v7x, 128 devices: a whole 4x4x4 slice. The times are simulated.
128 devices in a mesh: row: 8 (over y, core), col: 8 (over x_lo, z), feat: 2 (over x_hi).
Axes of the slice: x: 4 (x_hi: 2, x_lo: 2; x = x_hi * 2 + x_lo), y: 4, z: 4, core: 2. Of those that a mesh axis runs over, the one named last changes fastest.
Arguments:
- grad_out: bfloat16 [65536, 512], P(('row', 'col'), 'feat'), may hold values from -6 to 6
- saved_agg: bfloat16 [65536, 1024], P(('row', 'col'), 'feat'), may hold values from -0.119628906 to 0.119628906
- tile_values: bfloat16 [8, 8, 640, 128, 128], P('row', 'col'), may hold values from -0.0390625 to 0.0390625
- tile_rows: int32 [8, 8, 640], P('row', 'col'), may hold values from 0 to 63, as said below
- tile_cols: int32 [8, 8, 640], P('row', 'col'), may hold values from 0 to 63
- tile_counts: int32 [8, 8], P('row', 'col'), may hold values from 40 to 640, as said below
- weight: bfloat16 [1024, 512], replicated, may hold values from -0.25 to 0.25
Outputs:
- grad_in: bfloat16 [65536, 1024], P(('row', 'col', 'feat'))
- grad_weight: float32 [1024, 512], P('feat')
Inputs may be any that keep to these rules, and one draw needn't show every extreme that they name: `tile_counts`: some block has exactly 640 live slots and some block exactly 40. `tile_rows`: places may repeat within a block.
All inputs are finite; a program needn't handle non-finite values.
Results may differ from a plain program's by a relative error of at most 0.005.
Values may be sent and summed in bfloat16 or wider, within the bound.
A program may use at most 256 MiB of HBM per device.

v0:
```python
import jax
import jax.numpy as jnp
from jax import lax
from jax.sharding import PartitionSpec as P


def panel_sum(slot_values, slot_rows, slot_cols, live_mask, source, row_tiles):
    slot_total = slot_values.shape[0]
    tile_size = slot_values.shape[1]
    feat_width = source.shape[1]
    panels = source.reshape(source.shape[0] // tile_size, tile_size, feat_width)
    step_size = min(64, slot_total)

    def add_block(number, totals):
        offset = number * step_size
        block_values = lax.dynamic_slice_in_dim(slot_values, offset, step_size, 0)
        block_rows = lax.dynamic_slice_in_dim(slot_rows, offset, step_size, 0)
        block_cols = lax.dynamic_slice_in_dim(slot_cols, offset, step_size, 0)
        block_live = lax.dynamic_slice_in_dim(live_mask, offset, step_size, 0).astype(jnp.float32)
        picked = jnp.take(panels, block_cols, axis=0)
        products = jnp.einsum(
            "kab,kbf->kaf", block_values, picked, preferred_element_type=jnp.float32
        )
        return totals.at[block_rows].add(products * block_live[:, None, None])

    empty_sum = jnp.zeros((row_tiles, tile_size, feat_width), jnp.float32)
    totals = lax.fori_loop(0, slot_total // step_size, add_block, empty_sum)
    return totals.reshape(row_tiles * tile_size, feat_width)


def per_device(grad_out, saved_agg, tile_values, tile_rows, tile_cols, tile_counts, weight):
    tile_size = tile_values.shape[-1]
    slot_total = tile_values.shape[2]
    rows_dev = grad_out.shape[0]
    row_tiles = lax.axis_size("col") * (rows_dev // tile_size)
    depth_index = lax.axis_index("feat")
    slot_count = tile_counts[0, 0]
    full_feat = lax.all_gather(grad_out, "feat", axis=1, tiled=True)
    source = lax.all_gather(full_feat, "row", axis=0, tiled=True)
    paired_values = tile_values[0, 0].reshape(slot_total // 2, 2, tile_size, tile_size)
    own_values = lax.dynamic_index_in_dim(paired_values, depth_index, 1, False)
    own_rows = lax.dynamic_index_in_dim(
        tile_rows[0, 0].reshape(slot_total // 2, 2), depth_index, 1, False
    )
    own_cols = lax.dynamic_index_in_dim(
        tile_cols[0, 0].reshape(slot_total // 2, 2), depth_index, 1, False
    )
    live_mask = 2 * jnp.arange(slot_total // 2, dtype=jnp.int32) + depth_index < slot_count
    partial_value = panel_sum(own_values, own_rows, own_cols, live_mask, source, row_tiles)
    summed = lax.psum_scatter(partial_value, ("col", "feat"), scatter_dimension=0, tiled=True)
    hidden_grad = summed.astype(jnp.bfloat16)
    grad_in = lax.dot_general(
        hidden_grad, weight, (((1,), (1,)), ((), ())), preferred_element_type=jnp.float32
    ).astype(jnp.bfloat16)
    weight_term = lax.dot_general(
        saved_agg, full_feat, (((0,), (0,)), ((), ())), preferred_element_type=jnp.float32
    )
    grad_weight = lax.psum(weight_term, ("row", "col"))
    return (grad_in, grad_weight)


def solution(mesh):
    in_specs = (
        P(("row", "col"), "feat"),
        P(("row", "col"), "feat"),
        P("row", "col", None, None, None),
        P("row", "col", None),
        P("row", "col", None),
        P("row", "col"),
        P(),
    )
    out_specs = (P(("row", "col", "feat"), None), P("feat", None))
    return jax.shard_map(
        per_device, mesh=mesh, in_specs=in_specs, out_specs=out_specs, check_vma=False
    )
```

profile of v0, /device:TPU:0, one launch (start us, length us, event | category | flops | bytes accessed | tf_op | source)
XLA Modules:
  0.0 1302.7 jit_solution(9319648592536287447)
XLA Ops:
  7.2 0.0 copy-start
  7.2 0.0 all-gather.3.cloned.1.call-start
  7.2 0.7 all-gather.3.cloned.1.call-update
  7.9 0.0 all-gather.5.cloned.1.call-start
  8.0 29.5 %all-gather.3.cloned.1.call-done = bf16[1024,512]{1,0:T(8,128)(2,1)} async-done(((bf16[1024,256]{1,0:T(8,128)(2,1)}), bf16[1024,512]{1,0:T(8,128)(2,1)}) %all-gather.3.cloned.1.call-update) | async-done | bytes 1048592 | tf_op jit(solution)/shard_map/all_gather | solution.py:38
  37.4 0.0 all-gather.5.cloned.1.call-update
  37.5 0.0 reduce-scatter.2.cloned.1.call-start
  38.2 0.7 reduce
  38.9 0.7 reduce.2
  39.6 0.1 reshape_squeeze.11
  39.7 0.1 reshape_squeeze.9
  39.9 0.3 dynamic-slice_reduce_fusion
  40.2 13.0 %dynamic-slice_bitcast_fusion = bf16[320,128,128]{2,1,0:T(8,128)(2,1)} fusion(bf16[320,2,128,128]{3,2,1,0:T(8,128)(2,1)} %bitcast.14, s32[]{:T(128)S(6)} %select_n.41), kind=kLoop, calls=%fused_computation.14 | loop fusion | bytes 20971524 | tf_op jit(solution)/shard_map/jit(dynamic_index_in_dim)/squeeze | solution.py:41
  53.2 35.2 %all-gather.5.cloned.1.call-done = bf16[8192,512]{1,0:T(8,128)(2,1)} async-done(((bf16[1024,512]{1,0:T(8,128)(2,1)}), bf16[8192,512]{1,0:T(8,128)(2,1)}) %all-gather.5.cloned.1.call-update) | async-done | bytes 8388624 | tf_op jit(solution)/shard_map/all_gather | solution.py:39
  88.4 7.9 broadcast_in_dim.37
  96.2 291.6 %while.13 = (s32[]{:T(128)}, f32[64,128,512]{2,1,0:T(8,128)}, s32[320]{0:T(512)S(1)}, bf16[320,128,128]{2,1,0:T(8,128)(2,1)}, s32[320]{0:T(512)S(1)}, /*index=5*...) while((s32[]{:T(128)}, f32[64,128,512]{2,1,0:T(8,128)}, ...), condition=%wide.region_2.3_spmd, body=%wide.region_0.2_spmd.sunk | while | flops 1086326400 | bytes 94378600 | solution.py:27
  96.2 0.1 compare_select_fusion.4
  96.3 0.1 compare_and_fusion.2
  96.4 9.0 gather_fusion
  105.4 12.1 convolution_multiply_fusion.2
  117.6 37.2 %scatter_fusion = f32[64,128,512]{2,1,0:T(8,128)} fusion(f32[64,128,512]{2,1,0:T(8,128)} %get-tuple-element.207, s32[64]{0:T(128)S(1)} %compare_select_fusion.4, f32[64,128,512]{2,1,0:T(8,128)} %convolution_multiply_fusion.2), kind=kCustom, calls=%fused_computation.1.clone.1 | custom fusion | flops 4194304 | bytes 50331904 | tf_op jit(solution)/shard_map/while/body/eval_jaxpr/scatter-add | solution.py:24
  154.8 0.1 compare_select_fusion.4
  154.9 0.1 compare_and_fusion.2
  155.0 9.0 gather_fusion
  164.0 12.1 convolution_multiply_fusion.2
  176.1 36.9 %scatter_fusion = f32[64,128,512]{2,1,0:T(8,128)} fusion(f32[64,128,512]{2,1,0:T(8,128)} %get-tuple-element.207, s32[64]{0:T(128)S(1)} %compare_select_fusion.4, f32[64,128,512]{2,1,0:T(8,128)} %convolution_multiply_fusion.2), kind=kCustom, calls=%fused_computation.1.clone.1 | custom fusion | flops 4194304 | bytes 50331904 | tf_op jit(solution)/shard_map/while/body/eval_jaxpr/scatter-add | solution.py:24
  213.0 0.1 compare_select_fusion.4
  213.1 0.1 compare_and_fusion.2
  213.2 9.0 gather_fusion
  222.2 12.2 convolution_multiply_fusion.2
  234.4 36.7 %scatter_fusion = f32[64,128,512]{2,1,0:T(8,128)} fusion(f32[64,128,512]{2,1,0:T(8,128)} %get-tuple-element.207, s32[64]{0:T(128)S(1)} %compare_select_fusion.4, f32[64,128,512]{2,1,0:T(8,128)} %convolution_multiply_fusion.2), kind=kCustom, calls=%fused_computation.1.clone.1 | custom fusion | flops 4194304 | bytes 50331904 | tf_op jit(solution)/shard_map/while/body/eval_jaxpr/scatter-add | solution.py:24
  271.1 0.1 compare_select_fusion.4
  271.1 0.1 compare_and_fusion.2
  271.2 9.0 gather_fusion
  280.3 12.1 convolution_multiply_fusion.2
  292.4 36.9 %scatter_fusion = f32[64,128,512]{2,1,0:T(8,128)} fusion(f32[64,128,512]{2,1,0:T(8,128)} %get-tuple-element.207, s32[64]{0:T(128)S(1)} %compare_select_fusion.4, f32[64,128,512]{2,1,0:T(8,128)} %convolution_multiply_fusion.2), kind=kCustom, calls=%fused_computation.1.clone.1 | custom fusion | flops 4194304 | bytes 50331904 | tf_op jit(solution)/shard_map/while/body/eval_jaxpr/scatter-add | solution.py:24
  329.3 0.1 compare_select_fusion.4
  329.4 0.1 compare_and_fusion.2
  329.5 9.0 gather_fusion
  338.5 12.3 convolution_multiply_fusion.2
  350.8 37.1 %scatter_fusion = f32[64,128,512]{2,1,0:T(8,128)} fusion(f32[64,128,512]{2,1,0:T(8,128)} %get-tuple-element.207, s32[64]{0:T(128)S(1)} %compare_select_fusion.4, f32[64,128,512]{2,1,0:T(8,128)} %convolution_multiply_fusion.2), kind=kCustom, calls=%fused_computation.1.clone.1 | custom fusion | flops 4194304 | bytes 50331904 | tf_op jit(solution)/shard_map/while/body/eval_jaxpr/scatter-add | solution.py:24
  387.9 0.0 copy-start.1
  387.9 0.0 copy-start.2
  387.9 0.0 reduce-scatter.2.cloned.1.call-update
  387.9 0.0 all-reduce.2.cloned.1.call-start
  388.0 1.1 copy-done.1
  389.1 0.3 copy-done.2
  389.4 1.7 fusion.7
  391.1 0.0 all-reduce.2.cloned.1.call-update
  391.1 349.7 %reduce-scatter.2.cloned.1.call-done = f32[512,512]{1,0:T(8,128)} async-done(((f32[8192,512]{1,0:T(8,128)}), f32[512,512]{1,0:T(8,128)}) %reduce-scatter.2.cloned.1.call-update) | async-done | bytes 1048592 | tf_op jit(solution)/shard_map/reduce_scatter | solution.py:50
  740.8 0.0 copy-done
  740.8 2.9 convolution_convert_fusion
  743.8 550.1 %all-reduce.2.cloned.1.call-done = f32[512,512]{1,0:T(8,128)} async-done(((f32[512,512]{1,0:T(8,128)}), f32[512,512]{1,0:T(8,128)}) %all-reduce.2.cloned.1.call-update) | async-done | bytes 1048592 | tf_op jit(solution)/shard_map/psum | solution.py:58
  1293.9 2.3 copy.21
  (6 shorter events, 0.0 us)
Async XLA Ops:
  7.2 733.6 %copy-start = (bf16[1024,512]{1,0:T(8,128)(2,1)S(1)}, bf16[1024,512]{1,0:T(8,128)(2,1)}, u32[]{:S(2)}) copy-start(bf16[1024,512]{1,0:T(8,128)(2,1)} %param.15) | copy-start | bytes 3145732
  7.2 30.3 %all-gather.3.cloned.1.call-start = ((), (), s32[]{:S(2)}) async-start(), calls=%async_computation.1 | async-start | bytes 1572864 | tf_op jit(solution)/shard_map/all_gather | solution.py:38
  7.9 80.5 %all-gather.5.cloned.1.call-start = ((), (), s32[]{:S(2)}) async-start(), calls=%async_computation.2 | async-start | bytes 9437184 | tf_op jit(solution)/shard_map/all_gather | solution.py:39
  37.5 703.3 %reduce-scatter.2.cloned.1.call-start = ((), (), s32[]{:S(2)}) async-start(), calls=%async_computation.3 | async-start | bytes 17825792 | tf_op jit(solution)/shard_map/reduce_scatter | solution.py:50
  387.9 1.2 copy-start.1
  387.9 1.5 copy-start.2
  387.9 906.0 %all-reduce.2.cloned.1.call-start = ((), (), s32[]{:S(2)}) async-start(), calls=%async_computation.4 | async-start | bytes 2097152 | tf_op jit(solution)/shard_map/psum | solution.py:58
Sparse Core Ops, SparseCore 0:
  9.7 27.7 all-gather.2
  39.2 49.1 all-gather.4
  388.0 352.7 reduce-scatter.1
  743.7 550.1 all-reduce.1
where the time goes:
time: 1300 us
  waiting for transfers between devices  965 us (74%)
  other arithmetic  187 us (14%)
  local copies, waits for them, and re-layouts  70.4 us (5%)
  matrix products  65.5 us (5%)
  between operations  14.5 us (1%)
    psum x1, waiting for transfers between devices, per_device(): grad_weight = lax.psum(weight_term, ('row', 'col'))  550 us
    reduce_scatter x1, waiting for transfers between devices, per_device(): lax.psum_scatter(partial_value, ('col', 'feat'), scatter_dimension=0, til...  350 us
    scatter-add x5, other arithmetic, add_block(): return totals.at[block_rows].add(products * block_live[:, None, None])  185 us
    dot_general x5, matrix products, add_block(): jnp.einsum('kab,kbf->kaf', block_values, picked, preferred_element_type=j...  60.9 us
    gather x5, local copies, waits for them, and re-layouts, add_block(): picked = jnp.take(panels, block_cols, axis=0)  45.1 us
    all_gather x1, waiting for transfers between devices, per_device(): source = lax.all_gather(full_feat, 'row', axis=0, tiled=True)  35.2 us
    all_gather x1, waiting for transfers between devices, per_device(): full_feat = lax.all_gather(grad_out, 'feat', axis=1, tiled=True)  29.5 us
  transfers between devices with their start and end apart: 4, of which 4 were waited for; matrix products, arithmetic and copies ran while one was open for 2% of the time, Pallas kernels for 0%

commit v1 on v0

v1 whole, which is shorter than its diff:
```python
import functools

import jax
import jax.numpy as jnp
from jax import lax
from jax.experimental import pallas as pl
from jax.experimental.pallas import tpu as pltpu
from jax.sharding import PartitionSpec as P

MESH = pl.DeviceIdType.MESH
F32 = jnp.float32
BF16 = jnp.bfloat16

TILE = 128
ROW_TILES = 64
SLOTS = 640
STEPS = 384
UNROLL = 8
CHUNK = 40

XR = 224
ZR = 288
XH, ZH = XR // 2, ZR // 2


def neighbours():
    row, col, feat = (lax.axis_index(a) for a in ("row", "col", "feat"))
    return row, col, feat, row // 2, row % 2, col // 4, col % 4


def greet(devices):
    barrier = pltpu.get_barrier_semaphore()
    for d in devices:
        pl.semaphore_signal(barrier, inc=1, device_id=d, device_id_type=MESH)
    pl.semaphore_wait(barrier, len(devices))


def gather_kernel(x_ref, saved_ref, panel, gw_ref, other, ssem, rsem, lsem):
    row, col, feat, y, core, _, _ = neighbours()
    up = (((y + 1) % 4) * 2 + core, col, feat)
    down = (((y + 3) % 4) * 2 + core, col, feat)
    twin = (y * 2 + 1 - core, col, feat)
    mate = (row, col, 1 - feat)
    half = x_ref.shape[0] // 2
    lo, hi, whole = pl.ds(0, half), pl.ds(half, half), pl.ds(0, 2 * half)
    r_up, r_down, r_far = (((y + k) % 4) * 2 + core for k in (1, 3, 2))

    def send(i, src, r, part, to):
        return pltpu.make_async_remote_copy(
            src_ref=src.at[part],
            dst_ref=panel.at[r, part],
            send_sem=ssem.at[i],
            recv_sem=rsem.at[i],
            device_id=to,
            device_id_type=MESH,
        )

    greet((up, down, twin, mate))
    c = {}
    c[0] = send(0, x_ref, row, lo, up)
    c[1] = send(1, x_ref, row, hi, down)
    c[2] = send(2, x_ref, row, hi, up)
    c[3] = send(3, x_ref, row, lo, down)
    c[4] = send(4, x_ref, row, whole, twin)
    c[11] = pltpu.make_async_remote_copy(
        src_ref=x_ref, dst_ref=other, send_sem=ssem.at[11], recv_sem=rsem.at[11],
        device_id=mate, device_id_type=MESH,
    )
    for i in (0, 1, 11, 2, 3, 4):
        c[i].start()
    own = pltpu.make_async_copy(x_ref, panel.at[row], lsem.at[0])
    own.start()

    def term(source, slot):
        def columns(n, _):
            at = pl.ds(pl.multiple_of(n * 128, 128), 128)
            gw_ref[slot, at, :] = lax.dot_general(
                saved_ref[:, at], source[...], (((0,), (0,)), ((), ())),
                preferred_element_type=F32,
            ).astype(BF16)
            return 0

        lax.fori_loop(0, saved_ref.shape[1] // 128, columns, 0)

    c[0].wait_recv()
    c[5] = send(5, panel.at[r_down], r_down, lo, up)
    c[5].start()
    c[1].wait_recv()
    c[6] = send(6, panel.at[r_up], r_up, hi, down)
    c[6].start()
    term(x_ref, feat)
    c[2].wait_recv()
    c[7] = send(7, panel.at[r_down], r_down, whole, twin)
    c[7].start()
    c[3].wait_recv()
    c[8] = send(8, panel.at[r_up], r_up, whole, twin)
    c[8].start()
    c[5].wait_recv()
    c[9] = send(9, panel.at[r_far], r_far, lo, twin)
    c[9].start()
    c[6].wait_recv()
    c[10] = send(10, panel.at[r_far], r_far, hi, twin)
    c[10].start()
    c[11].wait_recv()
    term(other, 1 - feat)
    for i in (4, 7, 8, 9, 10):
        c[i].wait_recv()
    own.wait()
    for i in range(12):
        c[i].wait_send()


def gather(x, saved):
    rows, width = x.shape
    return pl.pallas_call(
        gather_kernel,
        out_shape=(
            jax.ShapeDtypeStruct((8, rows, width), BF16),
            jax.ShapeDtypeStruct((2, saved.shape[1], width), BF16),
        ),
        in_specs=[pl.BlockSpec(memory_space=pltpu.VMEM)] * 2,
        out_specs=(pl.BlockSpec(memory_space=pl.ANY), pl.BlockSpec(memory_space=pltpu.VMEM)),
        scratch_shapes=[
            pltpu.VMEM((rows, width), BF16),
            pltpu.SemaphoreType.DMA((12,)),
            pltpu.SemaphoreType.DMA((12,)),
            pltpu.SemaphoreType.DMA((1,)),
        ],
        compiler_params=pltpu.CompilerParams(
            collective_id=0, has_side_effects=True, vmem_limit_bytes=32 * 2**20
        ),
        name="gather",
    )(x, saved)


def product_kernel(word, info, size, tiles, panel, out, held, sems):
    count, steps = size[0], size[1]

    def chunk(n):
        at = pl.ds(n * CHUNK, CHUNK)
        return pltpu.make_async_copy(tiles.at[at], held.at[at], sems.at[n])

    for n in range(SLOTS // CHUNK):
        @pl.when(n * CHUNK < count)
        def _():
            chunk(n).start()

    held[SLOTS] = jnp.zeros((TILE, TILE), BF16)
    for n in range(SLOTS // CHUNK):
        @pl.when(n * CHUNK < count)
        def _():
            chunk(n).wait()

    def group(g, total):
        for u in range(UNROLL):
            p = g * UNROLL + u
            a, b, at = word[2 * p], word[2 * p + 1], info[p]
            left = jnp.concatenate([held[a // 64], held[b // 64]], axis=1)
            right = jnp.concatenate([panel[a % 64], panel[b % 64]], axis=0)
            fresh = jnp.dot(left, right, preferred_element_type=F32)
            total = fresh + jnp.where(at % 2 == 1, 0.0, total)
            out[at // 2] = total.astype(BF16)
        return total

    lax.fori_loop(
        0, (steps + UNROLL - 1) // UNROLL, group, jnp.zeros((TILE, panel.shape[2]), F32)
    )


def tile_products(word, info, size, tiles, panel):
    width = panel.shape[2]
    return pl.pallas_call(
        product_kernel,
        grid_spec=pltpu.PrefetchScalarGridSpec(
            num_scalar_prefetch=3,
            grid=(1,),
            in_specs=[
                pl.BlockSpec(memory_space=pl.ANY),
                pl.BlockSpec((ROW_TILES, TILE, width), lambda *_: (0, 0, 0)),
            ],
            out_specs=pl.BlockSpec((ROW_TILES, TILE, width), lambda *_: (0, 0, 0)),
            scratch_shapes=[
                pltpu.VMEM((SLOTS + 1, TILE, TILE), BF16),
                pltpu.SemaphoreType.DMA((SLOTS // CHUNK,)),
            ],
        ),
        out_shape=jax.ShapeDtypeStruct((ROW_TILES, TILE, width), BF16),
        compiler_params=pltpu.CompilerParams(vmem_limit_bytes=56 * 2**20),
        name="tile_products",
    )(word, info, size, tiles, panel)


def plan(rows, cols, count):
    slot = jnp.arange(SLOTS, dtype=jnp.int32)
    row = jnp.arange(ROW_TILES, dtype=jnp.int32)
    rows = jnp.where(slot < count, rows, ROW_TILES)
    held = jnp.sum((rows[None, :] == row[:, None]).astype(jnp.int32), axis=1)
    padded = jnp.maximum(held + held % 2, 2)
    end = jnp.sum(jnp.where(row[None, :] <= row[:, None], padded[None, :], 0), axis=1)
    start = end - padded
    before = jnp.sum(
        ((rows[None, :] == rows[:, None]) & (slot[None, :] < slot[:, None])).astype(jnp.int32), axis=1
    )
    first = jnp.sum(jnp.where(rows[:, None] == row[None, :], start[None, :], 0), axis=1)
    place = jnp.where(slot < count, first + before, 4 * STEPS)
    at = jnp.arange(2 * STEPS, dtype=jnp.int32)
    empty = SLOTS * 64
    word = empty + jnp.sum(
        jnp.where(place[None, :] == at[:, None], (slot * 64 + cols - empty)[None, :], 0), axis=1
    )
    step = 2 * jnp.arange(STEPS, dtype=jnp.int32)
    row_of = jnp.minimum(
        jnp.sum((end[None, :] <= step[:, None]).astype(jnp.int32), axis=1), ROW_TILES - 1
    )
    opens = jnp.sum((start[None, :] == step[:, None]).astype(jnp.int32), axis=1)
    size = jnp.stack([count, end[ROW_TILES - 1] // 2])
    return word, row_of * 2 + opens, size


def reduce_kernel(
    part, gw, weight, grad_in, grad_weight,
    z1p, z1m, z2p, z2m, zsp, zsm, xs, xr,
    xb, x1p, x1m, x2p, x2m, xw, xsp, xsm,
    give, got, kept, total,
    ar1, ar2s, ar2, ar3, ar4,
    ssem, rsem,
):
    row, col, feat, y, core, x, z = neighbours()
    zp, zm, zf = (z + 1) % 4, (z + 3) % 4, (z + 2) % 4
    up, down = (row, x * 4 + zp, feat), (row, x * 4 + zm, feat)
    twin = (row, (1 - x) * 4 + z, feat)
    cross = (row, (1 - x) * 4 + z, 1 - feat)
    others_r = [((row + j) % 8, col, feat) for j in range(1, 8)]
    others_c = [(row, (col + j) % 8, feat) for j in range(1, 8)]
    quarter = ((1 - x, feat), (x, 1 - feat), (x, feat), (1 - x, 1 - feat))
    r_x = pl.ds(0, XR)
    r_a, r_b = pl.ds(XR, ZH), pl.ds(XR + ZH, ZH)
    v_a, v_b = pl.ds(0, ZH), pl.ds(ZH, ZH)
    w_a, w_b = pl.ds(0, XH), pl.ds(XH, XH)
    started = []

    def send(src, dst, to):
        i = len(started)
        copy = pltpu.make_async_remote_copy(
            src_ref=src, dst_ref=dst, send_sem=ssem.at[i], recv_sem=rsem.at[i],
            device_id=to, device_id_type=MESH,
        )
        copy.start()
        started.append(copy)
        return copy

    def own(q, zz, rows):
        xx, h = quarter[q]
        return part.at[xx, zz, h, rows]

    def f32(ref):
        return ref[...].astype(F32)

    greet(others_r + others_c + [cross])

    hop_p, hop_m, plain_p, plain_m, sum_p, sum_m = {}, {}, {}, {}, {}, {}
    far = (zf, zp, zm, z)
    xhop = {}
    for k in range(2):
        xhop[0, k] = send(own(k, zf, r_x), xb.at[0, k], twin)
    for q in range(4):
        hop_p[q] = send(own(q, zf, r_a), z1p.at[q], up)
        hop_m[q] = send(own(q, zf, r_b), z1m.at[q], down)
    for o in range(1, 4):
        for k in range(2):
            xhop[o, k] = send(own(k, far[o], r_x), xb.at[o, k], twin)
    for q in range(4):
        plain_p[q] = send(own(q, zp, r_b), z2p.at[q, v_b], up)
        plain_m[q] = send(own(q, zm, r_a), z2m.at[q, v_a], down)
    ar1c = [send(gw.at[:, (row + j) % 8], ar1.at[j - 1], others_r[j - 1]) for j in range(1, 8)]

    for q in range(4):
        hop_p[q].wait_recv()
        zsp[q] = (f32(z1p.at[q]) + f32(own(q, zp, r_a))).astype(BF16)
        sum_p[q] = send(zsp.at[q], z2p.at[q, v_a], up)
        hop_m[q].wait_recv()
        zsm[q] = (f32(z1m.at[q]) + f32(own(q, zm, r_b))).astype(BF16)
        sum_m[q] = send(zsm.at[q], z2m.at[q, v_b], down)

    x1c = []
    for k in range(2):
        xhop[0, k].wait_recv()
        xw[k] = (f32(xb.at[0, k]) + f32(own(2 + k, zf, r_x))).astype(BF16)
        x1c.append((send(xw.at[k, w_a], x1p.at[k], up), send(xw.at[k, w_b], x1m.at[k], down)))

    for c in ar1c:
        c.wait_recv()
    acc = gw[:, row].astype(F32)
    for j in range(7):
        acc = acc + ar1[j].astype(F32)
    for s in range(8):
        ar2s[s] = acc[:, s * 8 : s * 8 + 8, :]
    ar2c = [send(ar2s.at[(col + j) % 8], ar2.at[j - 1], others_c[j - 1]) for j in range(1, 8)]

    x2c = []
    for k in range(2):
        xhop[1, k].wait_recv()
        x1c[k][0].wait_recv()
        mine = own(2 + k, zp, r_x)
        xsp[k, w_a] = (f32(xb.at[1, k, w_a]) + f32(mine.at[w_a]) + f32(x1p.at[k])).astype(BF16)
        xsp[k, w_b] = (f32(xb.at[1, k, w_b]) + f32(mine.at[w_b])).astype(BF16)
        up_copy = send(xsp.at[k], x2p.at[k], up)
        xhop[2, k].wait_recv()
        x1c[k][1].wait_recv()
        mine = own(2 + k, zm, r_x)
        xsm[k, w_a] = (f32(xb.at[2, k, w_a]) + f32(mine.at[w_a])).astype(BF16)
        xsm[k, w_b] = (f32(xb.at[2, k, w_b]) + f32(mine.at[w_b]) + f32(x1m.at[k])).astype(BF16)
        x2c.append((up_copy, send(xsm.at[k], x2m.at[k], down)))

    for c in ar2c:
        c.wait_recv()
    done = ar2s[col]
    for j in range(7):
        done = done + ar2[j]
    ar3[col] = done
    ar3c = [send(ar3.at[col], ar3.at[col], others_c[j]) for j in range(7)]

    def zsum(q):
        for c in (plain_p[q], plain_m[q], sum_p[q], sum_m[q]):
            c.wait_recv()
        return f32(own(q, z, pl.ds(XR, ZR))) + f32(z2p.at[q]) + f32(z2m.at[q])

    xc = []
    for k in range(2):
        xs[k] = zsum(k).astype(BF16)
        xc.append(send(xs.at[k], xr.at[k], twin))

    for c in ar3c:
        c.wait_recv()
    for s in range(8):
        total[:, s * 8 : s * 8 + 8, :] = ar3[s]
    ar4[row] = total[...].astype(BF16)
    ar4c = [send(ar4.at[row], ar4.at[row], others_r[j]) for j in range(7)]

    at_z = pl.ds(XR, ZR)
    z_kept = zsum(3)
    xc[1].wait_recv()
    give[at_z] = (z_kept + f32(xr.at[1])).astype(BF16)
    give_z = send(give.at[at_z], got.at[at_z], cross)
    z_kept = zsum(2)
    xc[0].wait_recv()
    kept[at_z] = (z_kept + f32(xr.at[0])).astype(BF16)

    def xsum(k):
        xhop[3, k].wait_recv()
        for c in x2c[k]:
            c.wait_recv()
        return f32(xb.at[3, k]) + f32(own(2 + k, z, r_x)) + f32(x2p.at[k]) + f32(x2m.at[k])

    give[r_x] = xsum(1).astype(BF16)
    give_x = send(give.at[r_x], got.at[r_x], cross)
    kept[r_x] = xsum(0).astype(BF16)

    for c in ar4c:
        c.wait_recv()
    for r in range(8):
        for f in range(2):
            grad_weight[r * 64 : r * 64 + 64, f * 256 : f * 256 + 256] = ar4[r, f].astype(F32)
    give_z.wait_recv()
    give_x.wait_recv()

    w_own = pl.ds(pl.multiple_of(feat * 256, 256), 256)
    w_other = pl.ds(pl.multiple_of((1 - feat) * 256, 256), 256)

    def columns(n, _):
        at = pl.ds(pl.multiple_of(n * 256, 256), 256)
        dims = (((1,), (1,)), ((), ()))
        value = lax.dot_general(kept[...], weight[at, w_own], dims, preferred_element_type=F32)
        value += lax.dot_general(got[...], weight[at, w_other], dims, preferred_element_type=F32)
        grad_in[:, at] = value.astype(BF16)
        return 0

    lax.fori_loop(0, weight.shape[0] // 256, columns, 0)
    for c in started:
        c.wait_send()


def reduce(part, gw, weight):
    vmem = pl.BlockSpec(memory_space=pltpu.VMEM)
    scratch = [
        ((4, ZH, 256), BF16), ((4, ZH, 256), BF16),
        ((4, ZR, 256), BF16), ((4, ZR, 256), BF16),
        ((4, ZH, 256), BF16), ((4, ZH, 256), BF16),
        ((2, ZR, 256), BF16), ((2, ZR, 256), BF16),
        ((4, 2, XR, 256), BF16),
        ((2, XH, 256), BF16), ((2, XH, 256), BF16),
        ((2, XR, 256), BF16), ((2, XR, 256), BF16),
        ((2, XR, 256), BF16), ((2, XR, 256), BF16), ((2, XR, 256), BF16),
        ((512, 256), BF16), ((512, 256), BF16), ((512, 256), BF16),
        ((2, 64, 256), F32),
        ((7, 2, 64, 256), BF16), ((8, 2, 8, 256), F32), ((7, 2, 8, 256), F32),
        ((8, 2, 8, 256), F32), ((8, 2, 64, 256), BF16),
    ]
    return pl.pallas_call(
        reduce_kernel,
        out_shape=(
            jax.ShapeDtypeStruct((512, 1024), BF16),
            jax.ShapeDtypeStruct((512, 512), F32),
        ),
        in_specs=[vmem] * 3,
        out_specs=(vmem, vmem),
        scratch_shapes=[pltpu.VMEM(s, t) for s, t in scratch]
        + [pltpu.SemaphoreType.DMA((80,)), pltpu.SemaphoreType.DMA((80,))],
        compiler_params=pltpu.CompilerParams(
            collective_id=1, has_side_effects=True, vmem_limit_bytes=48 * 2**20
        ),
        name="reduce",
    )(part, gw, weight)


def per_device(grad_out, saved_agg, tile_values, tile_rows, tile_cols, tile_counts, weight):
    word, info, size = plan(tile_rows[0, 0], tile_cols[0, 0], tile_counts[0, 0])
    panel, gw = gather(grad_out, saved_agg)
    part = tile_products(
        word, info, size, tile_values[0, 0], panel.reshape(ROW_TILES, TILE, grad_out.shape[1])
    )
    return reduce(
        part.reshape(2, 4, 2, 512, 256), gw.reshape(2, 8, 64, 256), weight
    )


def solution(mesh):
    in_specs = (
        P(("row", "col"), "feat"),
        P(("row", "col"), "feat"),
        P("row", "col", None, None, None),
        P("row", "col", None),
        P("row", "col", None),
        P("row", "col"),
        P(),
    )
    out_specs = (P(("row", "col", "feat"), None), P("feat", None))
    return jax.shard_map(
        per_device, mesh=mesh, in_specs=in_specs, out_specs=out_specs, check_vma=False
    )
```

time: 1300 us -> 117 us (0.09)
  the two profiles are of different devices: /device:TPU:0 before, /device:TPU:8 now
where the time goes in v1:
time: 117 us; the launch traced here: 116 us
  Pallas kernels  101 us (86%)
  local copies, waits for them, and re-layouts  6.72 us (6%)
  other arithmetic  4.17 us (4%)
  between operations  3.98 us (3%)
    pallas_call x1, Pallas kernels, reduce(): pl.pallas_call(reduce_kernel, out_shape=(jax.ShapeDtypeStruct((512, 1024)...  68.8 us
    pallas_call x1, Pallas kernels, gather(): pl.pallas_call(gather_kernel, out_shape=(jax.ShapeDtypeStruct((8, rows, w...  23.2 us
    pallas_call x1, Pallas kernels, tile_products(): pl.pallas_call(product_kernel, grid_spec=pltpu.PrefetchScalarGridSpec(num...  9.36 us
    unnamed x10, local copies, waits for them, and re-layouts  6.13 us

profile of v1, /device:TPU:8, one launch (start us, length us, event | category | flops | bytes accessed | tf_op | source)
XLA Modules:
  0.0 116.2 jit_solution(4168621214979570662)
XLA Ops:
  1.3 0.7 reduce.1
  2.0 0.1 convert_reduce_fusion.1
  2.1 0.1 select_reduce_fusion.2
  2.2 0.6 slice.3
  5.5 0.6 pad_add_fusion.size
  6.0 0.1 convert_reduce_fusion.3
  6.1 0.6 multiply_add_fusion.info
  6.7 0.1 select_reduce_fusion.1
  6.8 0.3 convert_reduce_fusion
  7.1 0.7 reduce.2
  7.8 0.3 select_reduce_fusion
  8.1 0.6 broadcast_add_fusion.word
  8.7 0.0 copy-start.1
  8.7 1.2 %copy-done.1 = bf16[1024,512]{1,0:T(8,128)(2,1)S(1)} copy-done((bf16[1024,512]{1,0:T(8,128)(2,1)S(1)}, bf16[1024,512]{1,0:T(8,128)(2,1)}, u32[]{:S(2)}) %copy-start.1) | copy-done | bytes 1048600
  9.9 0.0 copy-start.3
  9.9 1.0 copy-done.3
  11.0 23.2 %gather.1 = (bf16[8,1024,256]{2,1,0:T(8,128)(2,1)S(1)}, bf16[2,512,256]{2,1,0:T(8,128)(2,1)S(1)}) custom-call(bf16[1024,256]{1,0:T(8,128)(2,1)S(1)} %copy-done.3, bf16[1024,512]{1,0:T(8,128)(2,1)S(1)} %copy-done.1), custom_call_target="tpu_custom_call" | custom-call | tf_op jit(solution)/shard_map/gather/pallas_call | solution.py:115
  34.2 0.0 copy-start
  34.2 1.9 %copy-done = bf16[8,1024,256]{2,1,0:T(8,128)(2,1)} copy-done((bf16[8,1024,256]{2,1,0:T(8,128)(2,1)}, bf16[8,1024,256]{2,1,0:T(8,128)(2,1)S(1)}, u32[]{:S(2)}) %copy-start) | copy-done | bytes 4194328
  36.1 0.0 copy-start.2
  36.1 9.4 %tile_products.1 = bf16[64,128,256]{2,1,0:T(8,128)(2,1)} custom-call(s32[768]{0:T(1024)} %broadcast_add_fusion.word, s32[384]{0:T(512)} %multiply_add_fusion.info, s32[2]{0:T(128)} %pad_add_fusion.size, bf16[640,128,128]{2,1,0:T(8,128)(2,1)} %bitcast.13, bf16[64,128,256]{2,1,0:T(8,128)(2,1)} %bitcast.11), custom_call_target="tpu_custom_call" | custom-call | tf_op jit(solution)/shard_map/tile_products/pallas_call | solution.py:172
  45.5 0.0 copy-done.2
  45.5 68.8 %reduce.3 = (bf16[512,1024]{1,0:T(8,128)(2,1)S(1)}, f32[512,512]{1,0:T(8,128)S(1)}) custom-call(bf16[2,4,2,512,256]{4,3,2,1,0:T(8,128)(2,1)} %bitcast.14, bf16[2,8,64,256]{3,2,1,0:T(8,128)(2,1)S(1)} %bitcast.12, bf16[1024,512]{1,0:T(8,128)(2,1)S(1)} %copy-done.2), custom_call_target="tpu_custom_call" | custom-call | tf_op jit(solution)/shard_map/reduce/pallas_call | solution.py:399
  114.3 1.0 copy.12
  115.3 1.0 copy.13
  (5 shorter events, 0.0 us)
Async XLA Ops:
  8.7 1.2 %copy-start.1 = (bf16[1024,512]{1,0:T(8,128)(2,1)S(1)}, bf16[1024,512]{1,0:T(8,128)(2,1)}, u32[]{:S(2)}) copy-start(bf16[1024,512]{1,0:T(8,128)(2,1)} %saved_ref.1) | copy-start | bytes 3145732
  9.9 1.0 copy-start.3
  34.2 1.9 %copy-start = (bf16[8,1024,256]{2,1,0:T(8,128)(2,1)}, bf16[8,1024,256]{2,1,0:T(8,128)(2,1)S(1)}, u32[]{:S(2)}) copy-start(bf16[8,1024,256]{2,1,0:T(8,128)(2,1)S(1)} %get-tuple-element.4) | copy-start | bytes 12582916
  36.1 9.4 %copy-start.2 = (bf16[1024,512]{1,0:T(8,128)(2,1)S(1)}, bf16[1024,512]{1,0:T(8,128)(2,1)}, u32[]{:S(2)}) copy-start(bf16[1024,512]{1,0:T(8,128)(2,1)} %weight.1) | copy-start | bytes 3145732

commit v2 on v0

v2 whole, which is shorter than its diff:
```python
import jax
import jax.numpy as jnp
from jax import lax
from jax.experimental import pallas as pl
from jax.experimental.pallas import tpu as pltpu
from jax.sharding import PartitionSpec as P

MESH = pl.DeviceIdType.MESH
F32 = jnp.float32
BF16 = jnp.bfloat16
I32 = jnp.int32

TILE = 128
ROW_TILES = 64
SLOTS = 640
FOURS = 208
PLACES = 896
UNROLL = 16
CHUNKS = 16
WIDE = 128

XR = 224
ZR = 288
XH, ZH = XR // 2, ZR // 2
GIVE, KEEP = pl.ds(0, 2), pl.ds(2, 2)


def fused_kernel(
    rows_ref, cols_ref, count_ref, x_hbm, saved_hbm, tiles_hbm, weight_hbm,
    grad_in, grad_weight,
    held, panel0, panel1, slots, part,
    z1p, z1m, z2p, z2m, zsp, zsm, xs, xr, xb, x1p, x1m, x2p, x2m, xw, xsp, xsm,
    give, got, kept, saved, weight, other, gw, total_gw,
    ar1, ar2s, ar2, ar3, ar4,
    table_v, last_v, table, last,
    ssem, rsem, lsem,
):
    row, col, feat = (lax.axis_index(a) for a in ("row", "col", "feat"))
    y, core, x, z = row // 2, row % 2, col // 4, col % 4
    panels = (panel0, panel1)
    y_up = (((y + 1) % 4) * 2 + core, col, feat)
    y_down = (((y + 3) % 4) * 2 + core, col, feat)
    chip_mate = (y * 2 + 1 - core, col, feat)
    mate = (row, col, 1 - feat)
    up, down = (row, x * 4 + (z + 1) % 4, feat), (row, x * 4 + (z + 3) % 4, feat)
    twin = (row, (1 - x) * 4 + z, feat)
    cross = (row, (1 - x) * 4 + z, 1 - feat)
    others_r = [((row + j) % 8, col, feat) for j in range(1, 8)]
    others_c = [(row, (col + j) % 8, feat) for j in range(1, 8)]
    started = []

    def send(src, dst, to):
        i = len(started)
        copy = pltpu.make_async_remote_copy(
            src_ref=src, dst_ref=dst, send_sem=ssem.at[i], recv_sem=rsem.at[i],
            device_id=to, device_id_type=MESH,
        )
        copy.start()
        started.append(copy)
        return copy

    def f32(value):
        return value.astype(F32)

    local = []
    for h in range(2):
        local.append(
            pltpu.make_async_copy(
                x_hbm.at[:, :, pl.ds(h * WIDE, WIDE)], panels[h].at[pl.ds(row * 8, 8)], lsem.at[h]
            )
        )
    local.append(pltpu.make_async_copy(saved_hbm, saved, lsem.at[2]))
    local.append(pltpu.make_async_copy(weight_hbm, weight, lsem.at[3]))
    each = SLOTS // CHUNKS
    for n in range(CHUNKS):
        at = pl.ds(n * each, each)
        local.append(pltpu.make_async_copy(tiles_hbm.at[at], held.at[at], lsem.at[4 + n]))
    for c in local:
        c.start()

    barrier = pltpu.get_barrier_semaphore()
    friends = others_r + others_c + [mate, cross]
    for d in friends:
        pl.semaphore_signal(barrier, inc=1, device_id=d, device_id_type=MESH)
    pl.semaphore_wait(barrier, len(friends))

    r_down, r_up, r_far = (((y + k) % 4) * 2 + core for k in (3, 1, 2))

    def shard(h, r, half=None):
        at = pl.ds(r * 8, 8) if half is None else pl.ds(r * 8 + half * 4, 4)
        return panels[h].at[at]

    def pass_on(h, r, to, half=None):
        return send(shard(h, r, half), shard(h, r, half), to)

    ag = ({}, {})

    def gather_first(h):
        a = ag[h]
        a["up0"], a["down1"] = pass_on(h, row, y_up, 0), pass_on(h, row, y_down, 1)
        a["up1"], a["down0"] = pass_on(h, row, y_up, 1), pass_on(h, row, y_down, 0)
        a["core"] = pass_on(h, row, chip_mate)

    def gather_far(h):
        a = ag[h]
        a["up0"].wait_recv()
        a["far0"] = pass_on(h, r_down, y_up, 0)
        a["down1"].wait_recv()
        a["far1"] = pass_on(h, r_up, y_down, 1)

    def gather_near(h):
        a = ag[h]
        a["up1"].wait_recv()
        a["core_d"] = pass_on(h, r_down, chip_mate)
        a["down0"].wait_recv()
        a["core_u"] = pass_on(h, r_up, chip_mate)

    def gather_last(h):
        a = ag[h]
        a["far0"].wait_recv()
        a["core_f0"] = pass_on(h, r_far, chip_mate, 0)
        a["far1"].wait_recv()
        a["core_f1"] = pass_on(h, r_far, chip_mate, 1)

    def gather_end(h):
        for name in ("core", "core_d", "core_u", "core_f0", "core_f1"):
            ag[h][name].wait_recv()

    local[0].wait()
    gather_first(0)
    swap = [send(x_hbm.at[:, :, pl.ds(h * WIDE, WIDE)], other.at[h], mate) for h in range(2)]

    def iota(shape, axis):
        return lax.broadcasted_iota(I32, shape, axis)

    def total(mask, value, axis):
        return jnp.sum(jnp.where(mask, value, 0), axis=axis, keepdims=True)

    count = count_ref[0, 0]
    slot_r = iota((1, SLOTS), 1)
    slot_c = iota((SLOTS, 1), 0)
    eye = iota((SLOTS, SLOTS), 0) == iota((SLOTS, SLOTS), 1)
    rows_r = jnp.where(slot_r < count, rows_ref[...], ROW_TILES)
    rows_c = total(eye, rows_r, 1)
    cols_c = total(eye, cols_ref[...], 1)
    tile_r, tile_c = iota((1, TILE), 1), iota((TILE, 1), 0)
    n_c = total(rows_r == tile_c, 1, 1)
    n_r = total(rows_c == tile_r, 1, 0)
    n_c = jnp.where(tile_c < ROW_TILES, (n_c + 3) >> 2, 0)
    n_r = jnp.where(tile_r < ROW_TILES, (n_r + 3) >> 2, 0)
    end_r = total(tile_c <= tile_r, n_c, 0)
    start_r = end_r - n_r
    before = total((rows_r == rows_c) & (slot_r < slot_c), 1, 1)
    first = total(rows_c == tile_r, start_r, 1)
    place = jnp.where(rows_c < ROW_TILES, first * 4 + before, PLACES)
    at_r = iota((1, PLACES), 1)
    empty = SLOTS * 64
    word = total(place == at_r, slot_c * 64 + cols_c - empty, 0) + empty
    start_c = total(tile_c == tile_r, start_r, 1)
    opens = total((start_c * 4 == at_r) & (n_c > 0), 1, 0)
    table_v[...] = word + opens * 65536
    last_v[...] = jnp.where(n_r > 0, end_r - 1, FOURS)
    fill = [
        pltpu.make_async_copy(table_v, table, lsem.at[20]),
        pltpu.make_async_copy(last_v, last, lsem.at[21]),
    ]
    for c in fill:
        c.start()

    gather_far(0)
    local[1].wait()
    gather_first(1)

    def term(low, high, slot):
        def columns(n, _):
            at = pl.ds(pl.multiple_of(n * 128, 128), 128)
            source = jnp.concatenate([low().reshape(8 * TILE, WIDE), high().reshape(8 * TILE, WIDE)], axis=1)
            value = lax.dot_general(
                saved[:, at], source, (((0,), (0,)), ((), ())), preferred_element_type=F32
            )
            gw[slot, pl.ds(n * 2, 2)] = value.astype(BF16).reshape(2, 64, 256)
            return 0

        lax.fori_loop(0, 4, columns, 0)

    local[2].wait()
    mine = pl.ds(row * 8, 8)
    term(lambda: panel0[mine], lambda: panel1[mine], feat)
    gather_near(0)
    held[SLOTS] = jnp.zeros((TILE, TILE), BF16)
    slots[FOURS] = jnp.zeros((TILE, WIDE), BF16)
    for c in local[3:] + fill:
        c.wait()
    gather_last(0)
    gather_end(0)

    def products(h, lo, hi, sums):
        panel = panels[h]

        def group(g, sums):
            for u in range(UNROLL):
                p = g * UNROLL + u
                w = [table[0, 4 * p + i] for i in range(4)]
                left = jnp.concatenate([held[(a >> 6) & 1023] for a in w], axis=1)
                right = jnp.concatenate([panel[a & 63] for a in w], axis=0)
                fresh = jnp.dot(left, right, preferred_element_type=F32)
                sums = fresh + jnp.where((w[0] >> 16) > 0, 0.0, sums)
                slots[p] = sums.astype(BF16)
            return sums

        return lax.fori_loop(lo, hi, group, sums)

    quarters = ((1 - x, feat), (x, 1 - feat), (x, feat), (1 - x, 1 - feat))
    offsets = (2, 1, 3, 0)

    def collect(h):
        for o in range(4):
            for q in range(4):
                xx, half = quarters[q]
                base = (xx * 4 + (z + offsets[o]) % 4) * 8 + half * 4
                for t in range(4):
                    part[h, o, q, t * TILE : (t + 1) * TILE] = slots[last[0, base + t]]

    r_x, r_z = pl.ds(0, XR), pl.ds(XR, ZR)
    r_a, r_b = pl.ds(XR, ZH), pl.ds(XR + ZH, ZH)
    v_a, v_b = pl.ds(0, ZH), pl.ds(ZH, ZH)
    w_a, w_b = pl.ds(0, XH), pl.ds(XH, XH)
    rs = ({}, {})
    pair = (GIVE, KEEP)

    def xhop(h, o):
        rs[h]["xhop", o] = send(part.at[h, o, GIVE, r_x], xb.at[h, o], twin)

    def hop(h, g):
        s, at = rs[h], pair[g]
        s["hop_p", g] = send(part.at[h, 0, at, r_a], z1p.at[h, at], up)
        s["hop_m", g] = send(part.at[h, 0, at, r_b], z1m.at[h, at], down)

    def plain(h, g):
        s, at = rs[h], pair[g]
        s["plain_p", g] = send(part.at[h, 1, at, r_b], z2p.at[h, at, v_b], up)
        s["plain_m", g] = send(part.at[h, 2, at, r_a], z2m.at[h, at, v_a], down)

    def sums(h, g):
        s, at = rs[h], pair[g]
        s["hop_p", g].wait_recv()
        zsp[h, at] = (f32(z1p[h, at]) + f32(part[h, 1, at, r_a])).astype(BF16)
        s["sum_p", g] = send(zsp.at[h, at], z2p.at[h, at, v_a], up)
        s["hop_m", g].wait_recv()
        zsm[h, at] = (f32(z1m[h, at]) + f32(part[h, 2, at, r_b])).astype(BF16)
        s["sum_m", g] = send(zsm.at[h, at], z2m.at[h, at, v_b], down)

    def x_first(h):
        s = rs[h]
        s["xhop", 0].wait_recv()
        xw[h] = (f32(xb[h, 0]) + f32(part[h, 0, KEEP, r_x])).astype(BF16)
        s["x1p"] = send(xw.at[h, :, w_a], x1p.at[h], up)
        s["x1m"] = send(xw.at[h, :, w_b], x1m.at[h], down)

    def x_second(h):
        s = rs[h]
        s["xhop", 1].wait_recv()
        s["x1p"].wait_recv()
        xsp[h, :, w_a] = (
            f32(xb[h, 1, :, w_a]) + f32(part[h, 1, KEEP, w_a]) + f32(x1p[h])
        ).astype(BF16)
        xsp[h, :, w_b] = (f32(xb[h, 1, :, w_b]) + f32(part[h, 1, KEEP, w_b])).astype(BF16)
        s["x2p"] = send(xsp.at[h], x2p.at[h], up)
        s["xhop", 2].wait_recv()
        s["x1m"].wait_recv()
        xsm[h, :, w_a] = (f32(xb[h, 2, :, w_a]) + f32(part[h, 2, KEEP, w_a])).astype(BF16)
        xsm[h, :, w_b] = (
            f32(xb[h, 2, :, w_b]) + f32(part[h, 2, KEEP, w_b]) + f32(x1m[h])
        ).astype(BF16)
        s["x2m"] = send(xsm.at[h], x2m.at[h], down)

    def zsum(h, g):
        s, at = rs[h], pair[g]
        for name in ("plain_p", "plain_m", "sum_p", "sum_m"):
            s[name, g].wait_recv()
        return f32(part[h, 3, at, r_z]) + f32(z2p[h, at]) + f32(z2m[h, at])

    def z_given(h):
        xs[h] = zsum(h, 0).astype(BF16)
        rs[h]["xs"] = send(xs.at[h], xr.at[h], twin)
        xhop(h, 3)

    def lanes(h):
        return pl.ds(h * WIDE, WIDE)

    def z_done(h):
        s = rs[h]
        value = zsum(h, 1)
        s["xs"].wait_recv()
        value = (value + f32(xr[h])).astype(BF16)
        give[r_z, lanes(h)] = value[1]
        s["give_z"] = send(give.at[r_z, lanes(h)], got.at[r_z, lanes(h)], cross)
        kept[r_z, lanes(h)] = value[0]

    def x_done(h):
        s = rs[h]
        for name in (("xhop", 3), "x2p", "x2m"):
            s[name].wait_recv()
        value = (
            f32(xb[h, 3]) + f32(part[h, 3, KEEP, r_x]) + f32(x2p[h]) + f32(x2m[h])
        ).astype(BF16)
        give[r_x, lanes(h)] = value[1]
        s["give_x"] = send(give.at[r_x, lanes(h)], got.at[r_x, lanes(h)], cross)
        kept[r_x, lanes(h)] = value[0]

    def reduce_start(h):
        xhop(h, 0)
        hop(h, 0)
        hop(h, 1)
        xhop(h, 1)
        plain(h, 0)
        xhop(h, 2)

    def reduce_early(h):
        sums(h, 0)
        x_first(h)
        plain(h, 1)
        sums(h, 1)

    def weight_1():
        return [send(gw.at[:, (row + j) % 8], ar1.at[j - 1], others_r[j - 1]) for j in range(1, 8)]

    def weight_2(copies):
        for c in copies:
            c.wait_recv()
        acc = f32(gw[:, row])
        for j in range(7):
            acc = acc + f32(ar1[j])
        for s in range(8):
            ar2s[s] = acc[:, s * 8 : s * 8 + 8, :]
        return [send(ar2s.at[(col + j) % 8], ar2.at[j - 1], others_c[j - 1]) for j in range(1, 8)]

    def weight_3(copies):
        for c in copies:
            c.wait_recv()
        done = ar2s[col]
        for j in range(7):
            done = done + ar2[j]
        ar3[col] = done
        return [send(ar3.at[col], ar3.at[col], others_c[j]) for j in range(7)]

    def weight_4(copies):
        for c in copies:
            c.wait_recv()
        for s in range(8):
            total_gw[:, s * 8 : s * 8 + 8, :] = ar3[s]
        ar4[row] = total_gw[...].astype(BF16)
        return [send(ar4.at[row], ar4.at[row], others_r[j]) for j in range(7)]

    def weight_end(copies):
        for c in copies:
            c.wait_recv()
        for r in range(8):
            for f in range(2):
                grad_weight[r * 64 : r * 64 + 64, f * 256 : f * 256 + 256] = f32(ar4[r, f])

    zero = jnp.zeros((TILE, WIDE), F32)
    run = products(0, 0, 4, zero)
    gather_far(1)
    run = products(0, 4, 8, run)
    gather_near(1)
    products(0, 8, 13, run)
    gather_last(1)
    collect(0)
    reduce_start(0)
    for c in swap:
        c.wait_recv()
    term(lambda: other[0], lambda: other[1], 1 - feat)
    wc = weight_1()
    gather_end(1)
    run = products(1, 0, 2, zero)
    reduce_early(0)
    run = products(1, 2, 6, run)
    wc = weight_2(wc)
    z_given(0)
    x_second(0)
    run = products(1, 6, 10, run)
    wc = weight_3(wc)
    z_done(0)
    products(1, 10, 13, run)
    collect(1)
    reduce_start(1)
    x_done(0)
    wc = weight_4(wc)
    reduce_early(1)
    z_given(1)
    x_second(1)
    z_done(1)
    weight_end(wc)
    x_done(1)

    w_own = pl.ds(pl.multiple_of(feat * 256, 256), 256)
    w_other = pl.ds(pl.multiple_of((1 - feat) * 256, 256), 256)

    def finish(at_rows):
        def columns(n, _):
            at = pl.ds(pl.multiple_of(n * 256, 256), 256)
            dims = (((1,), (1,)), ((), ()))
            value = lax.dot_general(kept[at_rows], weight[at, w_own], dims, preferred_element_type=F32)
            value += lax.dot_general(got[at_rows], weight[at, w_other], dims, preferred_element_type=F32)
            grad_in[at_rows, at] = value.astype(BF16)
            return 0

        lax.fori_loop(0, 4, columns, 0)

    for h in range(2):
        rs[h]["give_z"].wait_recv()
    finish(r_z)
    for h in range(2):
        rs[h]["give_x"].wait_recv()
    finish(r_x)
    for c in started:
        c.wait_send()


COPIES = 2 * 11 + 2 + 2 * 23 + 28


def per_device(grad_out, saved_agg, tile_values, tile_rows, tile_cols, tile_counts, weight):
    vmem = pl.BlockSpec(memory_space=pltpu.VMEM)
    smem = pl.BlockSpec(memory_space=pltpu.SMEM)
    anywhere = pl.BlockSpec(memory_space=pl.ANY)
    scratch = [
        ((SLOTS + 1, TILE, TILE), BF16),
        ((64, TILE, WIDE), BF16), ((64, TILE, WIDE), BF16),
        ((FOURS + 1, TILE, WIDE), BF16), ((2, 4, 4, 512, WIDE), BF16),
        ((2, 4, ZH, WIDE), BF16), ((2, 4, ZH, WIDE), BF16),
        ((2, 4, ZR, WIDE), BF16), ((2, 4, ZR, WIDE), BF16),
        ((2, 4, ZH, WIDE), BF16), ((2, 4, ZH, WIDE), BF16),
        ((2, 2, ZR, WIDE), BF16), ((2, 2, ZR, WIDE), BF16),
        ((2, 4, 2, XR, WIDE), BF16),
        ((2, 2, XH, WIDE), BF16), ((2, 2, XH, WIDE), BF16),
        ((2, 2, XR, WIDE), BF16), ((2, 2, XR, WIDE), BF16),
        ((2, 2, XR, WIDE), BF16), ((2, 2, XR, WIDE), BF16), ((2, 2, XR, WIDE), BF16),
        ((512, 256), BF16), ((512, 256), BF16), ((512, 256), BF16),
        ((1024, 512), BF16), ((1024, 512), BF16), ((2, 8, TILE, WIDE), BF16),
        ((2, 8, 64, 256), BF16), ((2, 64, 256), F32),
        ((7, 2, 64, 256), BF16), ((8, 2, 8, 256), F32), ((7, 2, 8, 256), F32),
        ((8, 2, 8, 256), F32), ((8, 2, 64, 256), BF16),
        ((1, PLACES), I32), ((1, TILE), I32),
    ]
    return pl.pallas_call(
        fused_kernel,
        out_shape=(
            jax.ShapeDtypeStruct((512, 1024), BF16),
            jax.ShapeDtypeStruct((512, 512), F32),
        ),
        in_specs=[vmem, vmem, smem] + [anywhere] * 4,
        out_specs=(vmem, vmem),
        scratch_shapes=[pltpu.VMEM(s, t) for s, t in scratch]
        + [pltpu.SMEM((1, PLACES), I32), pltpu.SMEM((1, TILE), I32)]
        + [
            pltpu.SemaphoreType.DMA((COPIES,)),
            pltpu.SemaphoreType.DMA((COPIES,)),
            pltpu.SemaphoreType.DMA((22,)),
        ],
        compiler_params=pltpu.CompilerParams(
            collective_id=0, has_side_effects=True, vmem_limit_bytes=58 * 2**20
        ),
        name="fused",
    )(
        tile_rows[0], tile_cols[0], tile_counts,
        grad_out.reshape(8, TILE, 256), saved_agg, tile_values[0, 0], weight,
    )


def solution(mesh):
    in_specs = (
        P(("row", "col"), "feat"),
        P(("row", "col"), "feat"),
        P("row", "col", None, None, None),
        P("row", "col", None),
        P("row", "col", None),
        P("row", "col"),
        P(),
    )
    out_specs = (P(("row", "col", "feat"), None), P("feat", None))
    return jax.shard_map(
        per_device, mesh=mesh, in_specs=in_specs, out_specs=out_specs, check_vma=False
    )
```

time: 1300 us -> 79 us (0.06)
  waiting for transfers between devices: 965 us -> 0 us
  other arithmetic: 187 us -> 0 us
  Pallas kernels: 0 us -> 73 us
  local copies, waits for them, and re-layouts: 70.4 us -> 4.52 us
  matrix products: 65.5 us -> 0 us
  between operations: 14.5 us -> 1.29 us
    psum x1 -> x0, waiting for transfers between devices: 550 us -> none  [per_device(): grad_weight = lax.psum(weight_term, ('row', 'col'))]
    reduce_scatter x1 -> x0, waiting for transfers between devices: 350 us -> none  [per_device(): lax.psum_scatter(partial_value, ('col', 'feat'), scatter_dimension=0, til...]
    scatter-add x5 -> x0, other arithmetic: 185 us -> none  [add_block(): return totals.at[block_rows].add(products * block_live[:, None, None])]
    pallas_call x0 -> x1, Pallas kernels: none -> 73 us  [per_device(): pl.pallas_call(fused_kernel, out_shape=(jax.ShapeDtypeStruct((512, 1024),...]
    dot_general x7 -> x0, matrix products: 65.5 us -> none  [the longest x5 60.9 us: add_block(): jnp.einsum('kab,kbf->kaf', block_values, picked, preferred_element_type=j...]
    all_gather x2 -> x0, waiting for transfers between devices: 64.6 us -> none  [the longest x1 35.2 us: per_device(): source = lax.all_gather(full_feat, 'row', axis=0, tiled=True)]
    gather x5 -> x0, local copies, waits for them, and re-layouts: 45.1 us -> none  [add_block(): picked = jnp.take(panels, block_cols, axis=0)]
    squeeze x1 -> x0, local copies, waits for them, and re-layouts: 13 us -> none  [per_device(): own_values = lax.dynamic_index_in_dim(paired_values, depth_index, 1, False)]
  transfers between devices with their start and end apart: 4 -> 0, of which waited for: 4 -> 0; matrix products, arithmetic and copies ran while one was open for 2% -> 0% of each run, Pallas kernels for 0% -> 0%
where the time goes in v2:
time: 79 us; the launch traced here: 78.8 us
  Pallas kernels  73 us (92%)
  local copies, waits for them, and re-layouts  4.52 us (6%)
  between operations  1.29 us (2%)
    pallas_call x1, Pallas kernels, per_device(): pl.pallas_call(fused_kernel, out_shape=(jax.ShapeDtypeStruct((512, 1024),...  73 us
    unnamed x2, local copies, waits for them, and re-layouts  4.52 us

profile of v2, /device:TPU:0, one launch (start us, length us, event | category | flops | bytes accessed | tf_op | source)
XLA Modules:
  0.0 78.8 jit_solution(4699416810507739960)
XLA Ops:
  1.3 73.0 %fused.1 = (bf16[512,1024]{1,0:T(8,128)(2,1)}, f32[512,512]{1,0:T(8,128)}) custom-call(s32[1,640]{1,0:T(1,128)} %bitcast.6, s32[1,640]{1,0:T(1,128)} %bitcast.7, s32[1,1]{1,0:T(1,128)S(6)} %copy.11.count_ref, bf16[8,128,256]{2,1,0:T(8,128)(2,1)} %bitcast.5, bf16[1024,512]{1,0:T(8,128)(2,1)} %saved_hbm.1, bf16[640,128,128]{2,1,0:T(8,128)(2,1)} %bitcast.4, ...), custom_call_target="tpu_custom_call" | custom-call | tf_op jit(solution)/shard_map/fused/pallas_call | solution.py:447
  74.3 2.3 %copy.12 = bf16[512,1024]{1,0:T(8,128)(2,1)} copy(bf16[512,1024]{1,0:T(8,128)(2,1)} %get-tuple-element.4) | data formatting | bytes 2097152
  76.5 2.3 %copy.13 = f32[512,512]{1,0:T(8,128)} copy(f32[512,512]{1,0:T(8,128)} %get-tuple-element.5) | data formatting | bytes 2097152

commit v3 on v2

--- a/solution.py
+++ b/solution.py
@@ -13,9 +13,9 @@
 TILE = 128
 ROW_TILES = 64
 SLOTS = 640
-FOURS = 208
-PLACES = 896
-UNROLL = 16
+STEPS = 352
+PLACES = 768
+UNROLL = (88, 44)
 CHUNKS = 16
 WIDE = 128
 
@@ -26,13 +26,12 @@
 
 
 def fused_kernel(
-    rows_ref, cols_ref, count_ref, x_hbm, saved_hbm, tiles_hbm, weight_hbm,
-    grad_in, grad_weight,
+    rows_hbm, cols_hbm, count_hbm, x_hbm, saved_hbm, tiles_hbm,
+    hidden, ar4,
     held, panel0, panel1, slots, part,
     z1p, z1m, z2p, z2m, zsp, zsm, xs, xr, xb, x1p, x1m, x2p, x2m, xw, xsp, xsm,
-    give, got, kept, saved, weight, other, gw, total_gw,
-    ar1, ar2s, ar2, ar3, ar4,
-    table_v, last_v, table, last,
+    give, saved, other, gw, ar1, ar2s, ar2, ar3,
+    rows_ref, cols_ref, count_ref, table_v, last_v, table, last,
     ssem, rsem, lsem,
 ):
     row, col, feat = (lax.axis_index(a) for a in ("row", "col", "feat"))
@@ -69,13 +68,17 @@
                 x_hbm.at[:, :, pl.ds(h * WIDE, WIDE)], panels[h].at[pl.ds(row * 8, 8)], lsem.at[h]
             )
         )
+    tables = [
+        pltpu.make_async_copy(rows_hbm, rows_ref, lsem.at[22]),
+        pltpu.make_async_copy(cols_hbm, cols_ref, lsem.at[23]),
+        pltpu.make_async_copy(count_hbm, count_ref, lsem.at[24]),
+    ]
     local.append(pltpu.make_async_copy(saved_hbm, saved, lsem.at[2]))
-    local.append(pltpu.make_async_copy(weight_hbm, weight, lsem.at[3]))
     each = SLOTS // CHUNKS
     for n in range(CHUNKS):
         at = pl.ds(n * each, each)
-        local.append(pltpu.make_async_copy(tiles_hbm.at[at], held.at[at], lsem.at[4 + n]))
-    for c in local:
+        local.append(pltpu.make_async_copy(tiles_hbm.at[at], held.at[at], lsem.at[3 + n]))
+    for c in local[:2] + tables + local[2:]:
         c.start()
 
     barrier = pltpu.get_barrier_semaphore()
@@ -136,7 +139,9 @@
     def total(mask, value, axis):
         return jnp.sum(jnp.where(mask, value, 0), axis=axis, keepdims=True)
 
-    count = count_ref[0, 0]
+    for c in tables:
+        c.wait()
+    count = count_ref[...]
     slot_r = iota((1, SLOTS), 1)
     slot_c = iota((SLOTS, 1), 0)
     eye = iota((SLOTS, SLOTS), 0) == iota((SLOTS, SLOTS), 1)
@@ -146,20 +151,20 @@
     tile_r, tile_c = iota((1, TILE), 1), iota((TILE, 1), 0)
     n_c = total(rows_r == tile_c, 1, 1)
     n_r = total(rows_c == tile_r, 1, 0)
-    n_c = jnp.where(tile_c < ROW_TILES, (n_c + 3) >> 2, 0)
-    n_r = jnp.where(tile_r < ROW_TILES, (n_r + 3) >> 2, 0)
+    n_c = jnp.where(tile_c < ROW_TILES, (n_c + 1) >> 1, 0)
+    n_r = jnp.where(tile_r < ROW_TILES, (n_r + 1) >> 1, 0)
     end_r = total(tile_c <= tile_r, n_c, 0)
     start_r = end_r - n_r
     before = total((rows_r == rows_c) & (slot_r < slot_c), 1, 1)
     first = total(rows_c == tile_r, start_r, 1)
-    place = jnp.where(rows_c < ROW_TILES, first * 4 + before, PLACES)
+    place = jnp.where(rows_c < ROW_TILES, first * 2 + before, PLACES)
     at_r = iota((1, PLACES), 1)
     empty = SLOTS * 64
     word = total(place == at_r, slot_c * 64 + cols_c - empty, 0) + empty
     start_c = total(tile_c == tile_r, start_r, 1)
-    opens = total((start_c * 4 == at_r) & (n_c > 0), 1, 0)
+    opens = total((start_c * 2 == at_r) & (n_c > 0), 1, 0)
     table_v[...] = word + opens * 65536
-    last_v[...] = jnp.where(n_r > 0, end_r - 1, FOURS)
+    last_v[...] = jnp.where(n_r > 0, end_r - 1, STEPS)
     fill = [
         pltpu.make_async_copy(table_v, table, lsem.at[20]),
         pltpu.make_async_copy(last_v, last, lsem.at[21]),
@@ -188,7 +193,7 @@
     term(lambda: panel0[mine], lambda: panel1[mine], feat)
     gather_near(0)
     held[SLOTS] = jnp.zeros((TILE, TILE), BF16)
-    slots[FOURS] = jnp.zeros((TILE, WIDE), BF16)
+    slots[STEPS] = jnp.zeros((TILE, WIDE), BF16)
     for c in local[3:] + fill:
         c.wait()
     gather_last(0)
@@ -198,9 +203,9 @@
         panel = panels[h]
 
         def group(g, sums):
-            for u in range(UNROLL):
-                p = g * UNROLL + u
-                w = [table[0, 4 * p + i] for i in range(4)]
+            for u in range(UNROLL[h]):
+                p = g * UNROLL[h] + u
+                w = [table[0, 2 * p + i] for i in range(2)]
                 left = jnp.concatenate([held[(a >> 6) & 1023] for a in w], axis=1)
                 right = jnp.concatenate([panel[a & 63] for a in w], axis=0)
                 fresh = jnp.dot(left, right, preferred_element_type=F32)
@@ -230,6 +235,10 @@
 
     def xhop(h, o):
         rs[h]["xhop", o] = send(part.at[h, o, GIVE, r_x], xb.at[h, o], twin)
+
+    def xhop_own(h):
+        for k in (1, 0):
+            rs[h]["xhop", 3, k] = send(part.at[h, 3, k, r_x], xb.at[h, 3, k], twin)
 
     def hop(h, g):
         s, at = rs[h], pair[g]
@@ -265,14 +274,15 @@
             f32(xb[h, 1, :, w_a]) + f32(part[h, 1, KEEP, w_a]) + f32(x1p[h])
         ).astype(BF16)
         xsp[h, :, w_b] = (f32(xb[h, 1, :, w_b]) + f32(part[h, 1, KEEP, w_b])).astype(BF16)
-        s["x2p"] = send(xsp.at[h], x2p.at[h], up)
         s["xhop", 2].wait_recv()
         s["x1m"].wait_recv()
         xsm[h, :, w_a] = (f32(xb[h, 2, :, w_a]) + f32(part[h, 2, KEEP, w_a])).astype(BF16)
         xsm[h, :, w_b] = (
             f32(xb[h, 2, :, w_b]) + f32(part[h, 2, KEEP, w_b]) + f32(x1m[h])
         ).astype(BF16)
-        s["x2m"] = send(xsm.at[h], x2m.at[h], down)
+        for k in (1, 0):
+            s["x2p", k] = send(xsp.at[h, k], x2p.at[h, k], up)
+            s["x2m", k] = send(xsm.at[h, k], x2m.at[h, k], down)
 
     def zsum(h, g):
         s, at = rs[h], pair[g]
@@ -283,10 +293,13 @@
     def z_given(h):
         xs[h] = zsum(h, 0).astype(BF16)
         rs[h]["xs"] = send(xs.at[h], xr.at[h], twin)
-        xhop(h, 3)
+        xhop_own(h)
 
     def lanes(h):
         return pl.ds(h * WIDE, WIDE)
+
+    def features(h):
+        return pl.ds(pl.multiple_of(feat * 256 + h * WIDE, WIDE), WIDE)
 
     def z_done(h):
         s = rs[h]
@@ -294,19 +307,22 @@
         s["xs"].wait_recv()
         value = (value + f32(xr[h])).astype(BF16)
         give[r_z, lanes(h)] = value[1]
-        s["give_z"] = send(give.at[r_z, lanes(h)], got.at[r_z, lanes(h)], cross)
-        kept[r_z, lanes(h)] = value[0]
+        s["give_z"] = send(give.at[r_z, lanes(h)], hidden.at[r_z, features(h)], cross)
+        hidden[r_z, features(h)] = value[0]
 
     def x_done(h):
         s = rs[h]
-        for name in (("xhop", 3), "x2p", "x2m"):
-            s[name].wait_recv()
-        value = (
-            f32(xb[h, 3]) + f32(part[h, 3, KEEP, r_x]) + f32(x2p[h]) + f32(x2m[h])
-        ).astype(BF16)
-        give[r_x, lanes(h)] = value[1]
-        s["give_x"] = send(give.at[r_x, lanes(h)], got.at[r_x, lanes(h)], cross)
-        kept[r_x, lanes(h)] = value[0]
+        for k in (1, 0):
+            for name in (("xhop", 3, k), ("x2p", k), ("x2m", k)):
+                s[name].wait_recv()
+            value = (
+                f32(xb[h, 3, k]) + f32(part[h, 3, 2 + k, r_x]) + f32(x2p[h, k]) + f32(x2m[h, k])
+            ).astype(BF16)
+            if k == 1:
+                give[r_x, lanes(h)] = value
+                s["give_x"] = send(give.at[r_x, lanes(h)], hidden.at[r_x, features(h)], cross)
+            else:
+                hidden[r_x, features(h)] = value
 
     def reduce_start(h):
         xhop(h, 0)
@@ -317,118 +333,126 @@
         xhop(h, 2)
 
     def reduce_early(h):
-        sums(h, 0)
         x_first(h)
         plain(h, 1)
         sums(h, 1)
 
     def weight_1():
-        return [send(gw.at[:, (row + j) % 8], ar1.at[j - 1], others_r[j - 1]) for j in range(1, 8)]
+        return [send(gw.at[:, (col + j) % 8], ar1.at[j - 1], others_c[j - 1]) for j in range(1, 8)]
 
     def weight_2(copies):
         for c in copies:
             c.wait_recv()
-        acc = f32(gw[:, row])
+        acc = f32(gw[:, col])
         for j in range(7):
             acc = acc + f32(ar1[j])
-        for s in range(8):
-            ar2s[s] = acc[:, s * 8 : s * 8 + 8, :]
-        return [send(ar2s.at[(col + j) % 8], ar2.at[j - 1], others_c[j - 1]) for j in range(1, 8)]
+        for r in range(8):
+            ar2s[r] = acc[:, r * 8 : r * 8 + 8, :]
+        return [send(ar2s.at[(row + j) % 8], ar2.at[j - 1], others_r[j - 1]) for j in range(1, 8)]
 
     def weight_3(copies):
         for c in copies:
             c.wait_recv()
-        done = ar2s[col]
+        done = ar2s[row]
         for j in range(7):
             done = done + ar2[j]
-        ar3[col] = done
+        ar3[col] = done.reshape(16, 256).astype(BF16)
         return [send(ar3.at[col], ar3.at[col], others_c[j]) for j in range(7)]
 
     def weight_4(copies):
         for c in copies:
             c.wait_recv()
-        for s in range(8):
-            total_gw[:, s * 8 : s * 8 + 8, :] = ar3[s]
-        ar4[row] = total_gw[...].astype(BF16)
-        return [send(ar4.at[row], ar4.at[row], others_r[j]) for j in range(7)]
-
-    def weight_end(copies):
-        for c in copies:
-            c.wait_recv()
-        for r in range(8):
-            for f in range(2):
-                grad_weight[r * 64 : r * 64 + 64, f * 256 : f * 256 + 256] = f32(ar4[r, f])
+        ar4[row] = ar3[...]
+        return [send(ar3, ar4.at[row], others_r[j]) for j in range(7)]
 
     zero = jnp.zeros((TILE, WIDE), F32)
-    run = products(0, 0, 4, zero)
     gather_far(1)
-    run = products(0, 4, 8, run)
-    gather_near(1)
-    products(0, 8, 13, run)
-    gather_last(1)
-    collect(0)
-    reduce_start(0)
     for c in swap:
         c.wait_recv()
     term(lambda: other[0], lambda: other[1], 1 - feat)
     wc = weight_1()
+    run = products(0, 0, 2, zero)
+    gather_near(1)
+    products(0, 2, 4, run)
+    gather_last(1)
+    collect(0)
+    reduce_start(0)
+    wc = weight_2(wc)
     gather_end(1)
     run = products(1, 0, 2, zero)
+    sums(0, 0)
+    run = products(1, 2, 4, run)
     reduce_early(0)
-    run = products(1, 2, 6, run)
-    wc = weight_2(wc)
+    run = products(1, 4, 6, run)
+    wc = weight_3(wc)
     z_given(0)
+    products(1, 6, 8, run)
     x_second(0)
-    run = products(1, 6, 10, run)
-    wc = weight_3(wc)
-    z_done(0)
-    products(1, 10, 13, run)
     collect(1)
     reduce_start(1)
+    wc = weight_4(wc)
+    z_done(0)
     x_done(0)
-    wc = weight_4(wc)
+    sums(1, 0)
     reduce_early(1)
     z_given(1)
     x_second(1)
     z_done(1)
-    weight_end(wc)
+    for c in wc:
+        c.wait_recv()
     x_done(1)
-
-    w_own = pl.ds(pl.multiple_of(feat * 256, 256), 256)
-    w_other = pl.ds(pl.multiple_of((1 - feat) * 256, 256), 256)
-
-    def finish(at_rows):
-        def columns(n, _):
-            at = pl.ds(pl.multiple_of(n * 256, 256), 256)
-            dims = (((1,), (1,)), ((), ()))
-            value = lax.dot_general(kept[at_rows], weight[at, w_own], dims, preferred_element_type=F32)
-            value += lax.dot_general(got[at_rows], weight[at, w_other], dims, preferred_element_type=F32)
-            grad_in[at_rows, at] = value.astype(BF16)
-            return 0
-
-        lax.fori_loop(0, 4, columns, 0)
-
     for h in range(2):
         rs[h]["give_z"].wait_recv()
-    finish(r_z)
-    for h in range(2):
         rs[h]["give_x"].wait_recv()
-    finish(r_x)
     for c in started:
         c.wait_send()
 
 
-COPIES = 2 * 11 + 2 + 2 * 23 + 28
+def finish_kernel(hidden, weight, pieces, grad_in, grad_weight):
+    dims = (((1,), (1,)), ((), ()))
+    grad_in[...] = lax.dot_general(
+        hidden[...], weight[...], dims, preferred_element_type=F32
+    ).astype(BF16)
+    for s in range(2):
+        for r in range(8):
+            piece = pieces[r, s].astype(F32)
+            at = s * 64 + r * 8
+            for f in range(2):
+                grad_weight[at : at + 8, f * 256 : f * 256 + 256] = piece[f * 8 : f * 8 + 8]
+
+
+def finish(hidden, weight, pieces):
+    return pl.pallas_call(
+        finish_kernel,
+        grid=(4,),
+        in_specs=[
+            pl.BlockSpec((512, 512), lambda n: (0, 0)),
+            pl.BlockSpec((256, 512), lambda n: (n, 0)),
+            pl.BlockSpec((8, 2, 16, 256), lambda n: (0, n, 0, 0)),
+        ],
+        out_specs=(
+            pl.BlockSpec((512, 256), lambda n: (0, n)),
+            pl.BlockSpec((128, 512), lambda n: (n, 0)),
+        ),
+        out_shape=(
+            jax.ShapeDtypeStruct((512, 1024), BF16),
+            jax.ShapeDtypeStruct((512, 512), F32),
+        ),
+        compiler_params=pltpu.CompilerParams(vmem_limit_bytes=60 * 2**20),
+        name="finish",
+    )(hidden, weight, pieces)
+
+
+COPIES = 2 * 11 + 2 + 2 * 26 + 28
 
 
 def per_device(grad_out, saved_agg, tile_values, tile_rows, tile_cols, tile_counts, weight):
     vmem = pl.BlockSpec(memory_space=pltpu.VMEM)
-    smem = pl.BlockSpec(memory_space=pltpu.SMEM)
     anywhere = pl.BlockSpec(memory_space=pl.ANY)
     scratch = [
         ((SLOTS + 1, TILE, TILE), BF16),
         ((64, TILE, WIDE), BF16), ((64, TILE, WIDE), BF16),
-        ((FOURS + 1, TILE, WIDE), BF16), ((2, 4, 4, 512, WIDE), BF16),
+        ((STEPS + 1, TILE, WIDE), BF16), ((2, 4, 4, 512, WIDE), BF16),
         ((2, 4, ZH, WIDE), BF16), ((2, 4, ZH, WIDE), BF16),
         ((2, 4, ZR, WIDE), BF16), ((2, 4, ZR, WIDE), BF16),
         ((2, 4, ZH, WIDE), BF16), ((2, 4, ZH, WIDE), BF16),
@@ -437,36 +461,36 @@
         ((2, 2, XH, WIDE), BF16), ((2, 2, XH, WIDE), BF16),
         ((2, 2, XR, WIDE), BF16), ((2, 2, XR, WIDE), BF16),
         ((2, 2, XR, WIDE), BF16), ((2, 2, XR, WIDE), BF16), ((2, 2, XR, WIDE), BF16),
-        ((512, 256), BF16), ((512, 256), BF16), ((512, 256), BF16),
-        ((1024, 512), BF16), ((1024, 512), BF16), ((2, 8, TILE, WIDE), BF16),
-        ((2, 8, 64, 256), BF16), ((2, 64, 256), F32),
+        ((512, 256), BF16), ((1024, 512), BF16), ((2, 8, TILE, WIDE), BF16),
+        ((2, 8, 64, 256), BF16),
         ((7, 2, 64, 256), BF16), ((8, 2, 8, 256), F32), ((7, 2, 8, 256), F32),
-        ((8, 2, 8, 256), F32), ((8, 2, 64, 256), BF16),
-        ((1, PLACES), I32), ((1, TILE), I32),
+        ((8, 16, 256), BF16),
+        ((1, SLOTS), I32), ((1, SLOTS), I32), ((1, 1), I32), ((1, PLACES), I32), ((1, TILE), I32),
     ]
-    return pl.pallas_call(
+    hidden, pieces = pl.pallas_call(
         fused_kernel,
         out_shape=(
-            jax.ShapeDtypeStruct((512, 1024), BF16),
-            jax.ShapeDtypeStruct((512, 512), F32),
+            jax.ShapeDtypeStruct((512, 512), BF16),
+            jax.ShapeDtypeStruct((8, 8, 16, 256), BF16),
         ),
-        in_specs=[vmem, vmem, smem] + [anywhere] * 4,
+        in_specs=[anywhere] * 6,
         out_specs=(vmem, vmem),
         scratch_shapes=[pltpu.VMEM(s, t) for s, t in scratch]
         + [pltpu.SMEM((1, PLACES), I32), pltpu.SMEM((1, TILE), I32)]
         + [
             pltpu.SemaphoreType.DMA((COPIES,)),
             pltpu.SemaphoreType.DMA((COPIES,)),
-            pltpu.SemaphoreType.DMA((22,)),
+            pltpu.SemaphoreType.DMA((25,)),
         ],
         compiler_params=pltpu.CompilerParams(
-            collective_id=0, has_side_effects=True, vmem_limit_bytes=58 * 2**20
+            collective_id=0, has_side_effects=True, vmem_limit_bytes=56 * 2**20
         ),
         name="fused",
     )(
         tile_rows[0], tile_cols[0], tile_counts,
-        grad_out.reshape(8, TILE, 256), saved_agg, tile_values[0, 0], weight,
+        grad_out.reshape(8, TILE, 256), saved_agg, tile_values[0, 0],
     )
+    return finish(hidden, weight, pieces)
 
 
 def solution(mesh):

time: 79 us -> 71.2 us (0.901)
  local copies, waits for them, and re-layouts: 4.52 us -> 0 us
  Pallas kernels: 73 us -> 69.8 us
    unnamed x2 -> x0, local copies, waits for them, and re-layouts: 4.52 us -> none
    pallas_call x1 -> x2, Pallas kernels: 73 us -> 69.8 us  [the longest x1 65.4 us: per_device(): pl.pallas_call(fused_kernel, out_shape=(jax.ShapeDtypeStruct((512, 512),...]
where the time goes in v3:
time: 71.2 us; the launch traced here: 71.1 us
  Pallas kernels  69.8 us (98%)
  between operations  1.29 us (2%)
    pallas_call x1, Pallas kernels, per_device(): pl.pallas_call(fused_kernel, out_shape=(jax.ShapeDtypeStruct((512, 512),...  65.4 us
    pallas_call x1, Pallas kernels, finish(): pl.pallas_call(finish_kernel, grid=(4,), in_specs=[pl.BlockSpec((512, 512...  4.35 us

profile of v3, /device:TPU:0, one launch (start us, length us, event | category | flops | bytes accessed | tf_op | source)
XLA Modules:
  0.0 71.1 jit_solution(15322018478740265321)
XLA Ops:
  1.3 65.4 %fused.1 = (bf16[512,512]{1,0:T(8,128)(2,1)}, bf16[8,8,16,256]{3,2,1,0:T(8,128)(2,1)}) custom-call(s32[1,640]{1,0:T(1,128)} %bitcast.6, s32[1,640]{1,0:T(1,128)} %bitcast.7, s32[1,1]{1,0:T(1,128)S(6)} %copy.9.count_hbm, bf16[8,128,256]{2,1,0:T(8,128)(2,1)} %bitcast.5, bf16[1024,512]{1,0:T(8,128)(2,1)} %saved_hbm.1, bf16[640,128,128]{2,1,0:T(8,128)(2,1)} %bitcast.4), custom_call_target="tpu_custom_call" | custom-call | tf_op jit(solution)/shard_map/fused/pallas_call | solution.py:470
  66.7 4.3 %finish.1 = (bf16[512,1024]{1,0:T(8,128)(2,1)}, f32[512,512]{1,0:T(8,128)}) custom-call(bf16[512,512]{1,0:T(8,128)(2,1)} %get-tuple-element.4.hidden, bf16[1024,512]{1,0:T(8,128)(2,1)} %weight.1, bf16[8,8,16,256]{3,2,1,0:T(8,128)(2,1)} %get-tuple-element.5.pieces), custom_call_target="tpu_custom_call" | custom-call | tf_op jit(solution)/shard_map/finish/pallas_call | solution.py:425

commit v4 on v3

--- a/solution.py
+++ b/solution.py
@@ -27,10 +27,10 @@
 
 def fused_kernel(
     rows_hbm, cols_hbm, count_hbm, x_hbm, saved_hbm, tiles_hbm,
-    hidden, ar4,
+    hidden_hbm, pieces_hbm,
     held, panel0, panel1, slots, part,
     z1p, z1m, z2p, z2m, zsp, zsm, xs, xr, xb, x1p, x1m, x2p, x2m, xw, xsp, xsm,
-    give, saved, other, gw, ar1, ar2s, ar2, ar3,
+    give, hidden, saved, other, gw, ar1, ar2s, ar2, ar3, ar4,
     rows_ref, cols_ref, count_ref, table_v, last_v, table, last,
     ssem, rsem, lsem,
 ):
@@ -60,6 +60,11 @@
 
     def f32(value):
         return value.astype(F32)
+
+    barrier = pltpu.get_barrier_semaphore()
+    friends = others_r + others_c + [mate, cross]
+    for d in friends:
+        pl.semaphore_signal(barrier, inc=1, device_id=d, device_id_type=MESH)
 
     local = []
     for h in range(2):
@@ -80,11 +85,6 @@
         local.append(pltpu.make_async_copy(tiles_hbm.at[at], held.at[at], lsem.at[3 + n]))
     for c in local[:2] + tables + local[2:]:
         c.start()
-
-    barrier = pltpu.get_barrier_semaphore()
-    friends = others_r + others_c + [mate, cross]
-    for d in friends:
-        pl.semaphore_signal(barrier, inc=1, device_id=d, device_id_type=MESH)
     pl.semaphore_wait(barrier, len(friends))
 
     r_down, r_up, r_far = (((y + k) % 4) * 2 + core for k in (3, 1, 2))
@@ -218,8 +218,8 @@
     quarters = ((1 - x, feat), (x, 1 - feat), (x, feat), (1 - x, 1 - feat))
     offsets = (2, 1, 3, 0)
 
-    def collect(h):
-        for o in range(4):
+    def collect(h, first, end):
+        for o in range(first, end):
             for q in range(4):
                 xx, half = quarters[q]
                 base = (xx * 4 + (z + offsets[o]) % 4) * 8 + half * 4
@@ -325,9 +325,11 @@
                 hidden[r_x, features(h)] = value
 
     def reduce_start(h):
+        collect(h, 0, 1)
         xhop(h, 0)
         hop(h, 0)
         hop(h, 1)
+        collect(h, 1, 4)
         xhop(h, 1)
         plain(h, 0)
         xhop(h, 2)
@@ -375,7 +377,6 @@
     gather_near(1)
     products(0, 2, 4, run)
     gather_last(1)
-    collect(0)
     reduce_start(0)
     wc = weight_2(wc)
     gather_end(1)
@@ -388,7 +389,6 @@
     z_given(0)
     products(1, 6, 8, run)
     x_second(0)
-    collect(1)
     reduce_start(1)
     wc = weight_4(wc)
     z_done(0)
@@ -400,44 +400,72 @@
     z_done(1)
     for c in wc:
         c.wait_recv()
+    out = [pltpu.make_async_copy(ar4, pieces_hbm, lsem.at[0])]
+    out[0].start()
     x_done(1)
-    for h in range(2):
-        rs[h]["give_z"].wait_recv()
-        rs[h]["give_x"].wait_recv()
+    for at, name in ((r_z, "give_z"), (r_x, "give_x")):
+        for h in range(2):
+            rs[h][name].wait_recv()
+        out.append(pltpu.make_async_copy(hidden.at[at], hidden_hbm.at[at], lsem.at[len(out)]))
+        out[-1].start()
+    for c in out:
+        c.wait()
     for c in started:
         c.wait_send()
 
 
-def finish_kernel(hidden, weight, pieces, grad_in, grad_weight):
+def finish_kernel(
+    hidden, weight, pieces, grad_in, grad_weight, hidden_v, weight_v, pieces_v, left, right, sems
+):
+    copies = [pltpu.make_async_copy(hidden, hidden_v, sems.at[0])]
+    blocks = [pl.ds(n * 256, 256) for n in range(4)]
+    for n, at in enumerate(blocks):
+        copies.append(pltpu.make_async_copy(weight.at[at], weight_v.at[at], sems.at[1 + n]))
+    copies.append(pltpu.make_async_copy(pieces, pieces_v, sems.at[5]))
+    for c in copies:
+        c.start()
+    copies[0].wait()
     dims = (((1,), (1,)), ((), ()))
-    grad_in[...] = lax.dot_general(
-        hidden[...], weight[...], dims, preferred_element_type=F32
-    ).astype(BF16)
-    for s in range(2):
-        for r in range(8):
-            piece = pieces[r, s].astype(F32)
-            at = s * 64 + r * 8
-            for f in range(2):
-                grad_weight[at : at + 8, f * 256 : f * 256 + 256] = piece[f * 8 : f * 8 + 8]
+    out = []
+    for n, at in enumerate(blocks):
+        copies[1 + n].wait()
+        left[:, at] = lax.dot_general(
+            hidden_v[...], weight_v[at], dims, preferred_element_type=F32
+        ).astype(BF16)
+        out.append(pltpu.make_async_copy(left.at[:, at], grad_in.at[:, at], sems.at[6 + n]))
+        out[-1].start()
+        if n == 2:
+            copies[5].wait()
+            for s in range(8):
+                for r in range(8):
+                    piece = pieces_v[r, s].astype(F32)
+                    rows = s * 64 + r * 8
+                    for f in range(2):
+                        right[rows : rows + 8, f * 256 : f * 256 + 256] = piece[f * 8 : f * 8 + 8]
+            out.append(pltpu.make_async_copy(right, grad_weight, sems.at[10]))
+            out[-1].start()
+    for c in out:
+        c.wait()
 
 
 def finish(hidden, weight, pieces):
+    anywhere = pl.BlockSpec(memory_space=pl.ANY)
     return pl.pallas_call(
         finish_kernel,
-        grid=(4,),
-        in_specs=[
-            pl.BlockSpec((512, 512), lambda n: (0, 0)),
-            pl.BlockSpec((256, 512), lambda n: (n, 0)),
-            pl.BlockSpec((8, 2, 16, 256), lambda n: (0, n, 0, 0)),
-        ],
-        out_specs=(
-            pl.BlockSpec((512, 256), lambda n: (0, n)),
-            pl.BlockSpec((128, 512), lambda n: (n, 0)),
-        ),
+        in_specs=[anywhere] * 3,
+        out_specs=(anywhere, anywhere),
         out_shape=(
             jax.ShapeDtypeStruct((512, 1024), BF16),
             jax.ShapeDtypeStruct((512, 512), F32),
         ),
+        scratch_shapes=[
+            pltpu.VMEM((512, 512), BF16),
+            pltpu.VMEM((1024, 512), BF16),
+            pltpu.VMEM((8, 8, 16, 256), BF16),
+            pltpu.VMEM((512, 1024), BF16),
+            pltpu.VMEM((512, 512), F32),
+            pltpu.SemaphoreType.DMA((11,)),
+        ],
         compiler_params=pltpu.CompilerParams(vmem_limit_bytes=60 * 2**20),
         name="finish",
     )(hidden, weight, pieces)
@@ -447,7 +475,6 @@
 
 
 def per_device(grad_out, saved_agg, tile_values, tile_rows, tile_cols, tile_counts, weight):
-    vmem = pl.BlockSpec(memory_space=pltpu.VMEM)
     anywhere = pl.BlockSpec(memory_space=pl.ANY)
     scratch = [
         ((SLOTS + 1, TILE, TILE), BF16),
@@ -461,10 +488,10 @@
         ((2, 2, XH, WIDE), BF16), ((2, 2, XH, WIDE), BF16),
         ((2, 2, XR, WIDE), BF16), ((2, 2, XR, WIDE), BF16),
         ((2, 2, XR, WIDE), BF16), ((2, 2, XR, WIDE), BF16), ((2, 2, XR, WIDE), BF16),
-        ((512, 256), BF16), ((1024, 512), BF16), ((2, 8, TILE, WIDE), BF16),
+        ((512, 256), BF16), ((512, 512), BF16), ((1024, 512), BF16), ((2, 8, TILE, WIDE), BF16),
         ((2, 8, 64, 256), BF16),
         ((7, 2, 64, 256), BF16), ((8, 2, 8, 256), F32), ((7, 2, 8, 256), F32),
-        ((8, 16, 256), BF16),
+        ((8, 16, 256), BF16), ((8, 8, 16, 256), BF16),
         ((1, SLOTS), I32), ((1, SLOTS), I32), ((1, 1), I32), ((1, PLACES), I32), ((1, TILE), I32),
     ]
     hidden, pieces = pl.pallas_call(
@@ -474,7 +501,7 @@
             jax.ShapeDtypeStruct((8, 8, 16, 256), BF16),
         ),
         in_specs=[anywhere] * 6,
-        out_specs=(vmem, vmem),
+        out_specs=(anywhere, anywhere),
         scratch_shapes=[pltpu.VMEM(s, t) for s, t in scratch]
         + [pltpu.SMEM((1, PLACES), I32), pltpu.SMEM((1, TILE), I32)]
         + [

time: 71.2 us -> 70 us (0.983)
  Pallas kernels: 69.8 us -> 68.5 us
where the time goes in v4:
time: 70 us; the launch traced here: 69.8 us
  Pallas kernels  68.5 us (98%)
  between operations  1.29 us (2%)
    pallas_call x1, Pallas kernels, per_device(): pl.pallas_call(fused_kernel, out_shape=(jax.ShapeDtypeStruct((512, 512),...  64.7 us
    pallas_call x1, Pallas kernels, finish(): pl.pallas_call(finish_kernel, in_specs=[anywhere] * 3, out_specs=(anywher...  3.8 us

profile of v4, /device:TPU:0, one launch (start us, length us, event | category | flops | bytes accessed | tf_op | source)
XLA Modules:
  0.0 69.8 jit_solution(3065898352200150665)
XLA Ops:
  1.3 64.7 %fused.1 = (bf16[512,512]{1,0:T(8,128)(2,1)}, bf16[8,8,16,256]{3,2,1,0:T(8,128)(2,1)}) custom-call(s32[1,640]{1,0:T(1,128)} %bitcast.6, s32[1,640]{1,0:T(1,128)} %bitcast.7, s32[1,1]{1,0:T(1,128)S(6)} %copy.9.count_hbm, bf16[8,128,256]{2,1,0:T(8,128)(2,1)} %bitcast.5, bf16[1024,512]{1,0:T(8,128)(2,1)} %saved_hbm.1, bf16[640,128,128]{2,1,0:T(8,128)(2,1)} %bitcast.4), custom_call_target="tpu_custom_call" | custom-call | tf_op jit(solution)/shard_map/fused/pallas_call | solution.py:497
  66.0 3.8 %finish.1 = (bf16[512,1024]{1,0:T(8,128)(2,1)}, f32[512,512]{1,0:T(8,128)}) custom-call(bf16[512,512]{1,0:T(8,128)(2,1)} %get-tuple-element.4.hidden, bf16[1024,512]{1,0:T(8,128)(2,1)} %weight.1, bf16[8,8,16,256]{3,2,1,0:T(8,128)(2,1)} %get-tuple-element.5.pieces), custom_call_target="tpu_custom_call" | custom-call | tf_op jit(solution)/shard_map/finish/pallas_call | solution.py:453

commit v5 on v4

--- a/solution.py
+++ b/solution.py
@@ -30,7 +30,7 @@
     hidden_hbm, pieces_hbm,
     held, panel0, panel1, slots, part,
     z1p, z1m, z2p, z2m, zsp, zsm, xs, xr, xb, x1p, x1m, x2p, x2m, xw, xsp, xsm,
-    give, hidden, saved, other, gw, ar1, ar2s, ar2, ar3, ar4,
+    give, hidden, x_v, saved, other, gw, ar1, ar2s, ar2, ar3, ar4,
     rows_ref, cols_ref, count_ref, table_v, last_v, table, last,
     ssem, rsem, lsem,
 ):
@@ -66,24 +66,20 @@
     for d in friends:
         pl.semaphore_signal(barrier, inc=1, device_id=d, device_id_type=MESH)
 
-    local = []
-    for h in range(2):
-        local.append(
-            pltpu.make_async_copy(
-                x_hbm.at[:, :, pl.ds(h * WIDE, WIDE)], panels[h].at[pl.ds(row * 8, 8)], lsem.at[h]
-            )
-        )
+    local = [
+        pltpu.make_async_copy(x_hbm, x_v, lsem.at[0]),
+        pltpu.make_async_copy(saved_hbm, saved, lsem.at[1]),
+    ]
     tables = [
         pltpu.make_async_copy(rows_hbm, rows_ref, lsem.at[22]),
         pltpu.make_async_copy(cols_hbm, cols_ref, lsem.at[23]),
         pltpu.make_async_copy(count_hbm, count_ref, lsem.at[24]),
     ]
-    local.append(pltpu.make_async_copy(saved_hbm, saved, lsem.at[2]))
     each = SLOTS // CHUNKS
     for n in range(CHUNKS):
         at = pl.ds(n * each, each)
-        local.append(pltpu.make_async_copy(tiles_hbm.at[at], held.at[at], lsem.at[3 + n]))
-    for c in local[:2] + tables + local[2:]:
+        local.append(pltpu.make_async_copy(tiles_hbm.at[at], held.at[at], lsem.at[2 + n]))
+    for c in local[:1] + tables + local[1:]:
         c.start()
     pl.semaphore_wait(barrier, len(friends))
 
@@ -129,9 +125,12 @@
         for name in ("core", "core_d", "core_u", "core_f0", "core_f1"):
             ag[h][name].wait_recv()
 
+    mine = pl.ds(row * 8, 8)
     local[0].wait()
+    panel0[mine] = x_v[:, :, :WIDE]
     gather_first(0)
-    swap = [send(x_hbm.at[:, :, pl.ds(h * WIDE, WIDE)], other.at[h], mate) for h in range(2)]
+    panel1[mine] = x_v[:, :, WIDE:]
+    swap = [send(shard(h, row), other.at[h], mate) for h in range(2)]
 
     def iota(shape, axis):
         return lax.broadcasted_iota(I32, shape, axis)
@@ -173,7 +172,6 @@
         c.start()
 
     gather_far(0)
-    local[1].wait()
     gather_first(1)
 
     def term(low, high, slot):
@@ -188,13 +186,12 @@
 
         lax.fori_loop(0, 4, columns, 0)
 
-    local[2].wait()
-    mine = pl.ds(row * 8, 8)
+    local[1].wait()
     term(lambda: panel0[mine], lambda: panel1[mine], feat)
     gather_near(0)
     held[SLOTS] = jnp.zeros((TILE, TILE), BF16)
     slots[STEPS] = jnp.zeros((TILE, WIDE), BF16)
-    for c in local[3:] + fill:
+    for c in local[2:] + fill:
         c.wait()
     gather_last(0)
     gather_end(0)
@@ -231,14 +228,10 @@
     v_a, v_b = pl.ds(0, ZH), pl.ds(ZH, ZH)
     w_a, w_b = pl.ds(0, XH), pl.ds(XH, XH)
     rs = ({}, {})
-    pair = (GIVE, KEEP)
+    pair = (GIVE, pl.ds(3, 1), pl.ds(2, 1))
 
     def xhop(h, o):
         rs[h]["xhop", o] = send(part.at[h, o, GIVE, r_x], xb.at[h, o], twin)
-
-    def xhop_own(h):
-        for k in (1, 0):
-            rs[h]["xhop", 3, k] = send(part.at[h, 3, k, r_x], xb.at[h, 3, k], twin)
 
     def hop(h, g):
         s, at = rs[h], pair[g]
@@ -266,23 +259,24 @@
         s["x1p"] = send(xw.at[h, :, w_a], x1p.at[h], up)
         s["x1m"] = send(xw.at[h, :, w_b], x1m.at[h], down)
 
-    def x_second(h):
+    def x_second(h, k):
         s = rs[h]
-        s["xhop", 1].wait_recv()
-        s["x1p"].wait_recv()
-        xsp[h, :, w_a] = (
-            f32(xb[h, 1, :, w_a]) + f32(part[h, 1, KEEP, w_a]) + f32(x1p[h])
-        ).astype(BF16)
-        xsp[h, :, w_b] = (f32(xb[h, 1, :, w_b]) + f32(part[h, 1, KEEP, w_b])).astype(BF16)
-        s["xhop", 2].wait_recv()
-        s["x1m"].wait_recv()
-        xsm[h, :, w_a] = (f32(xb[h, 2, :, w_a]) + f32(part[h, 2, KEEP, w_a])).astype(BF16)
-        xsm[h, :, w_b] = (
-            f32(xb[h, 2, :, w_b]) + f32(part[h, 2, KEEP, w_b]) + f32(x1m[h])
-        ).astype(BF16)
-        for k in (1, 0):
-            s["x2p", k] = send(xsp.at[h, k], x2p.at[h, k], up)
-            s["x2m", k] = send(xsm.at[h, k], x2m.at[h, k], down)
+        if k == 1:
+            s["xhop", 1].wait_recv()
+        if k == 1:
+            s["x1p"].wait_recv()
+        own = part[h, 1, 2 + k, r_x]
+        xsp[h, k, w_a] = (f32(xb[h, 1, k, w_a]) + f32(own[:XH]) + f32(x1p[h, k])).astype(BF16)
+        xsp[h, k, w_b] = (f32(xb[h, 1, k, w_b]) + f32(own[XH:])).astype(BF16)
+        s["x2p", k] = send(xsp.at[h, k], x2p.at[h, k], up)
+        if k == 1:
+            s["xhop", 2].wait_recv()
+        if k == 1:
+            s["x1m"].wait_recv()
+        own = part[h, 2, 2 + k, r_x]
+        xsm[h, k, w_a] = (f32(xb[h, 2, k, w_a]) + f32(own[:XH])).astype(BF16)
+        xsm[h, k, w_b] = (f32(xb[h, 2, k, w_b]) + f32(own[XH:]) + f32(x1m[h, k])).astype(BF16)
+        s["x2m", k] = send(xsm.at[h, k], x2m.at[h, k], down)
 
     def zsum(h, g):
         s, at = rs[h], pair[g]
@@ -292,8 +286,9 @@
 
     def z_given(h):
         xs[h] = zsum(h, 0).astype(BF16)
-        rs[h]["xs"] = send(xs.at[h], xr.at[h], twin)
-        xhop_own(h)
+        for k in (1, 0):
+            rs[h]["xs", k] = send(xs.at[h, k], xr.at[h, k], twin)
+            rs[h]["xhop", 3, k] = send(part.at[h, 3, k, r_x], xb.at[h, 3, k], twin)
 
     def lanes(h):
         return pl.ds(h * WIDE, WIDE)
@@ -301,43 +296,43 @@
     def features(h):
         return pl.ds(pl.multiple_of(feat * 256 + h * WIDE, WIDE), WIDE)
 
-    def z_done(h):
+    def z_done(h, k):
         s = rs[h]
-        value = zsum(h, 1)
-        s["xs"].wait_recv()
-        value = (value + f32(xr[h])).astype(BF16)
-        give[r_z, lanes(h)] = value[1]
-        s["give_z"] = send(give.at[r_z, lanes(h)], hidden.at[r_z, features(h)], cross)
-        hidden[r_z, features(h)] = value[0]
-
-    def x_done(h):
+        value = zsum(h, 2 - k)[0]
+        s["xs", k].wait_recv()
+        value = (value + f32(xr[h, k])).astype(BF16)
+        if k == 1:
+            give[r_z, lanes(h)] = value
+            s["give_z"] = send(give.at[r_z, lanes(h)], hidden.at[r_z, features(h)], cross)
+        else:
+            hidden[r_z, features(h)] = value
+
+    def x_done(h, k):
         s = rs[h]
-        for k in (1, 0):
-            for name in (("xhop", 3, k), ("x2p", k), ("x2m", k)):
-                s[name].wait_recv()
-            value = (
-                f32(xb[h, 3, k]) + f32(part[h, 3, 2 + k, r_x]) + f32(x2p[h, k]) + f32(x2m[h, k])
-            ).astype(BF16)
-            if k == 1:
-                give[r_x, lanes(h)] = value
-                s["give_x"] = send(give.at[r_x, lanes(h)], hidden.at[r_x, features(h)], cross)
-            else:
-                hidden[r_x, features(h)] = value
+        for name in (("xhop", 3, k), ("x2p", k), ("x2m", k)):
+            s[name].wait_recv()
+        value = (
+            f32(xb[h, 3, k]) + f32(part[h, 3, 2 + k, r_x]) + f32(x2p[h, k]) + f32(x2m[h, k])
+        ).astype(BF16)
+        if k == 1:
+            give[r_x, lanes(h)] = value
+            s["give_x"] = send(give.at[r_x, lanes(h)], hidden.at[r_x, features(h)], cross)
+        else:
+            hidden[r_x, features(h)] = value
 
     def reduce_start(h):
         collect(h, 0, 1)
         xhop(h, 0)
-        hop(h, 0)
-        hop(h, 1)
+        for g in range(3):
+            hop(h, g)
         collect(h, 1, 4)
         xhop(h, 1)
         plain(h, 0)
         xhop(h, 2)
 
-    def reduce_early(h):
-        x_first(h)
-        plain(h, 1)
-        sums(h, 1)
+    def kept(h, k):
+        plain(h, 2 - k)
+        sums(h, 2 - k)
 
     def weight_1():
         return [send(gw.at[:, (col + j) % 8], ar1.at[j - 1], others_c[j - 1]) for j in range(1, 8)]
@@ -383,26 +378,36 @@
     run = products(1, 0, 2, zero)
     sums(0, 0)
     run = products(1, 2, 4, run)
-    reduce_early(0)
+    x_first(0)
+    kept(0, 1)
+    kept(0, 0)
     run = products(1, 4, 6, run)
     wc = weight_3(wc)
     z_given(0)
     products(1, 6, 8, run)
-    x_second(0)
+    x_second(0, 1)
+    x_second(0, 0)
     reduce_start(1)
     wc = weight_4(wc)
-    z_done(0)
-    x_done(0)
+    z_done(0, 1)
+    z_done(0, 0)
+    x_done(0, 1)
+    x_done(0, 0)
     sums(1, 0)
-    reduce_early(1)
+    x_first(1)
+    kept(1, 1)
     z_given(1)
-    x_second(1)
-    z_done(1)
+    x_second(1, 1)
+    kept(1, 0)
+    x_second(1, 0)
+    z_done(1, 1)
+    x_done(1, 1)
+    z_done(1, 0)
     for c in wc:
         c.wait_recv()
     out = [pltpu.make_async_copy(ar4, pieces_hbm, lsem.at[0])]
     out[0].start()
-    x_done(1)
+    x_done(1, 0)
     for at, name in ((r_z, "give_z"), (r_x, "give_x")):
         for h in range(2):
             rs[h][name].wait_recv()
@@ -471,7 +476,7 @@
     )(hidden, weight, pieces)
 
 
-COPIES = 2 * 11 + 2 + 2 * 26 + 28
+COPIES = 2 * 11 + 2 + 2 * 33 + 28
 
 
 def per_device(grad_out, saved_agg, tile_values, tile_rows, tile_cols, tile_counts, weight):
@@ -488,7 +493,7 @@
         ((2, 2, XH, WIDE), BF16), ((2, 2, XH, WIDE), BF16),
         ((2, 2, XR, WIDE), BF16), ((2, 2, XR, WIDE), BF16),
         ((2, 2, XR, WIDE), BF16), ((2, 2, XR, WIDE), BF16), ((2, 2, XR, WIDE), BF16),
-        ((512, 256), BF16), ((512, 512), BF16), ((1024, 512), BF16), ((2, 8, TILE, WIDE), BF16),
+        ((512, 256), BF16), ((512, 512), BF16), ((8, TILE, 256), BF16), ((1024, 512), BF16), ((2, 8, TILE, WIDE), BF16),
         ((2, 8, 64, 256), BF16),
         ((7, 2, 64, 256), BF16), ((8, 2, 8, 256), F32), ((7, 2, 8, 256), F32),
         ((8, 16, 256), BF16), ((8, 8, 16, 256), BF16),

time: 70 us -> 69.2 us (0.989)
  Pallas kernels: 68.5 us -> 67.8 us
    pallas_call x1, Pallas kernels: 64.7 us -> 64 us  [per_device(): pl.pallas_call(fused_kernel, out_shape=(jax.ShapeDtypeStruct((512, 512),...]
where the time goes in v5:
time: 69.2 us; the launch traced here: 69.1 us
  Pallas kernels  67.8 us (98%)
  between operations  1.29 us (2%)
    pallas_call x1, Pallas kernels, per_device(): pl.pallas_call(fused_kernel, out_shape=(jax.ShapeDtypeStruct((512, 512),...  64 us
    pallas_call x1, Pallas kernels, finish(): pl.pallas_call(finish_kernel, in_specs=[anywhere] * 3, out_specs=(anywher...  3.8 us

profile of v5, /device:TPU:0, one launch (start us, length us, event | category | flops | bytes accessed | tf_op | source)
XLA Modules:
  0.0 69.1 jit_solution(13906253139420500839)
XLA Ops:
  1.3 64.0 %fused.1 = (bf16[512,512]{1,0:T(8,128)(2,1)}, bf16[8,8,16,256]{3,2,1,0:T(8,128)(2,1)}) custom-call(s32[1,640]{1,0:T(1,128)} %bitcast.6, s32[1,640]{1,0:T(1,128)} %bitcast.7, s32[1,1]{1,0:T(1,128)S(6)} %copy.9.count_hbm, bf16[8,128,256]{2,1,0:T(8,128)(2,1)} %bitcast.5, bf16[1024,512]{1,0:T(8,128)(2,1)} %saved_hbm.1, bf16[640,128,128]{2,1,0:T(8,128)(2,1)} %bitcast.4), custom_call_target="tpu_custom_call" | custom-call | tf_op jit(solution)/shard_map/fused/pallas_call | solution.py:502
  65.3 3.8 %finish.1 = (bf16[512,1024]{1,0:T(8,128)(2,1)}, f32[512,512]{1,0:T(8,128)}) custom-call(bf16[512,512]{1,0:T(8,128)(2,1)} %get-tuple-element.4.hidden, bf16[1024,512]{1,0:T(8,128)(2,1)} %weight.1, bf16[8,8,16,256]{3,2,1,0:T(8,128)(2,1)} %get-tuple-element.5.pieces), custom_call_target="tpu_custom_call" | custom-call | tf_op jit(solution)/shard_map/finish/pallas_call | solution.py:458

commit v6 on v5

--- a/solution.py
+++ b/solution.py
@@ -427,8 +427,8 @@
     for n, at in enumerate(blocks):
         copies.append(pltpu.make_async_copy(weight.at[at], weight_v.at[at], sems.at[1 + n]))
     copies.append(pltpu.make_async_copy(pieces, pieces_v, sems.at[5]))
-    for c in copies:
-        c.start()
+    for i in (0, 1, 5, 2, 3, 4):
+        copies[i].start()
     copies[0].wait()
     dims = (((1,), (1,)), ((), ()))
     out = []
@@ -439,7 +439,7 @@
         ).astype(BF16)
         out.append(pltpu.make_async_copy(left.at[:, at], grad_in.at[:, at], sems.at[6 + n]))
         out[-1].start()
-        if n == 2:
+        if n == 0:
             copies[5].wait()
             for s in range(8):
                 for r in range(8):

time: 69.2 us -> 69.2 us (level)
  no operation moved by 1% of the time
where the time goes in v6:
time: 69.2 us; the launch traced here: 69.1 us
  Pallas kernels  67.8 us (98%)
  between operations  1.29 us (2%)
    pallas_call x1, Pallas kernels, per_device(): pl.pallas_call(fused_kernel, out_shape=(jax.ShapeDtypeStruct((512, 512),...  64 us
    pallas_call x1, Pallas kernels, finish(): pl.pallas_call(finish_kernel, in_specs=[anywhere] * 3, out_specs=(anywher...  3.8 us

profile of v6, /device:TPU:0, one launch (start us, length us, event | category | flops | bytes accessed | tf_op | source)
XLA Modules:
  0.0 69.1 jit_solution(15537477334188501430)
XLA Ops:
  1.3 64.0 %fused.1 = (bf16[512,512]{1,0:T(8,128)(2,1)}, bf16[8,8,16,256]{3,2,1,0:T(8,128)(2,1)}) custom-call(s32[1,640]{1,0:T(1,128)} %bitcast.6, s32[1,640]{1,0:T(1,128)} %bitcast.7, s32[1,1]{1,0:T(1,128)S(6)} %copy.9.count_hbm, bf16[8,128,256]{2,1,0:T(8,128)(2,1)} %bitcast.5, bf16[1024,512]{1,0:T(8,128)(2,1)} %saved_hbm.1, bf16[640,128,128]{2,1,0:T(8,128)(2,1)} %bitcast.4), custom_call_target="tpu_custom_call" | custom-call | tf_op jit(solution)/shard_map/fused/pallas_call | solution.py:502
  65.3 3.8 %finish.1 = (bf16[512,1024]{1,0:T(8,128)(2,1)}, f32[512,512]{1,0:T(8,128)}) custom-call(bf16[512,512]{1,0:T(8,128)(2,1)} %get-tuple-element.4.hidden, bf16[1024,512]{1,0:T(8,128)(2,1)} %weight.1, bf16[8,8,16,256]{3,2,1,0:T(8,128)(2,1)} %get-tuple-element.5.pieces), custom_call_target="tpu_custom_call" | custom-call | tf_op jit(solution)/shard_map/finish/pallas_call | solution.py:458

commit v7 on v6

--- a/solution.py
+++ b/solution.py
@@ -373,10 +373,10 @@
     products(0, 2, 4, run)
     gather_last(1)
     reduce_start(0)
-    wc = weight_2(wc)
     gather_end(1)
     run = products(1, 0, 2, zero)
     sums(0, 0)
+    wc = weight_2(wc)
     run = products(1, 2, 4, run)
     x_first(0)
     kept(0, 1)

time: 69.2 us -> 70 us (1.012)
  Pallas kernels: 67.8 us -> 68.5 us
    pallas_call x1, Pallas kernels: 64 us -> 64.7 us  [per_device(): pl.pallas_call(fused_kernel, out_shape=(jax.ShapeDtypeStruct((512, 512),...]
where the time goes in v7:
time: 70 us; the launch traced here: 69.8 us
  Pallas kernels  68.5 us (98%)
  between operations  1.29 us (2%)
    pallas_call x1, Pallas kernels, per_device(): pl.pallas_call(fused_kernel, out_shape=(jax.ShapeDtypeStruct((512, 512),...  64.7 us
    pallas_call x1, Pallas kernels, finish(): pl.pallas_call(finish_kernel, in_specs=[anywhere] * 3, out_specs=(anywher...  3.8 us

profile of v7, /device:TPU:0, one launch (start us, length us, event | category | flops | bytes accessed | tf_op | source)
XLA Modules:
  0.0 69.8 jit_solution(12251273718440649412)
XLA Ops:
  1.3 64.7 %fused.1 = (bf16[512,512]{1,0:T(8,128)(2,1)}, bf16[8,8,16,256]{3,2,1,0:T(8,128)(2,1)}) custom-call(s32[1,640]{1,0:T(1,128)} %bitcast.6, s32[1,640]{1,0:T(1,128)} %bitcast.7, s32[1,1]{1,0:T(1,128)S(6)} %copy.9.count_hbm, bf16[8,128,256]{2,1,0:T(8,128)(2,1)} %bitcast.5, bf16[1024,512]{1,0:T(8,128)(2,1)} %saved_hbm.1, bf16[640,128,128]{2,1,0:T(8,128)(2,1)} %bitcast.4), custom_call_target="tpu_custom_call" | custom-call | tf_op jit(solution)/shard_map/fused/pallas_call | solution.py:502
  66.0 3.8 %finish.1 = (bf16[512,1024]{1,0:T(8,128)(2,1)}, f32[512,512]{1,0:T(8,128)}) custom-call(bf16[512,512]{1,0:T(8,128)(2,1)} %get-tuple-element.4.hidden, bf16[1024,512]{1,0:T(8,128)(2,1)} %weight.1, bf16[8,8,16,256]{3,2,1,0:T(8,128)(2,1)} %get-tuple-element.5.pieces), custom_call_target="tpu_custom_call" | custom-call | tf_op jit(solution)/shard_map/finish/pallas_call | solution.py:458
